TPU v7x, 256 devices: a whole 4x4x8 slice. The times are simulated.
256 devices in a mesh: dp: 64 (over x, z, core), mp: 4 (over y).
Axes of the slice: x: 4, y: 4, z: 8, core: 2. Of those that a mesh axis runs over, the one named last changes fastest.
Arguments:
- features: bfloat16 [65536, 1024], P('dp'), may hold values from -6 to 6
- out_grads: bfloat16 [65536, 4, 1024], P('dp', None, 'mp'), may hold values from -0.0234375 to 0.0234375
- norm_grads: float32 [64, 2048], P('dp'), may hold values from -0.75 to 0.75
- owners: int32 [5], replicated, may hold values from 0 to 63, as said below
- moment1: float32 [4, 1024, 1024], P(None, 'dp', 'mp'), may hold values from -6 to 6
- moment2: float32 [4, 1024, 1024], P(None, 'dp', 'mp'), may hold values from 0.1 to 10
- left_stats: float32 [4, 1024, 1024], P(None, 'dp', 'mp'), may hold values from -1024 to 1024, as said below
- right_stats: float32 [4, 1024, 1024], P(None, 'dp', 'mp'), may hold values from -1024 to 1024, as said below
- left_basis: float32 [4, 1024, 1024], P(None, 'dp', 'mp'), may hold values from -1 to 2
- right_basis: float32 [4, 1024, 1024], P(None, 'dp', 'mp'), may hold values from -1 to 2
- norm_m: float32 [2048], P('dp'), may hold values from -6 to 6
- norm_v: float32 [2048], P('dp'), may hold values from 0.1 to 10
Outputs:
- new_moment1: float32 [4, 1024, 1024], P(None, 'dp', 'mp')
- new_moment2: float32 [4, 1024, 1024], P(None, 'dp', 'mp')
- new_left_stats: float32 [4, 1024, 1024], P(None, 'dp', 'mp')
- new_right_stats: float32 [4, 1024, 1024], P(None, 'dp', 'mp')
- new_left_basis: float32 [4, 1024, 1024], P(None, 'dp', 'mp')
- new_right_basis: float32 [4, 1024, 1024], P(None, 'dp', 'mp')
- update_slots: bfloat16 [64, 1024, 1024], P('dp', None, 'mp')
- new_norm_m: float32 [2048], P('dp')
- new_norm_v: float32 [2048], P('dp')
- norm_slots: float32 [64, 2048], P('dp')
Inputs may be any that keep to these rules, and one draw needn't show every extreme that they name: `owners`: the first 4 entries are distinct, so a dp index owns at most one tile; the last entry may equal any of them. `left_stats`: each tile of statistics is symmetric. `right_stats`: each tile of statistics is symmetric.
All inputs are finite; a program needn't handle non-finite values.
Results may differ from a plain program's by a relative error of at most 0.0072.
Values may be sent and summed in bfloat16 or wider, within the bound.
No kernel may reach another device: no remote copies, remote signals or barrier semaphores. Data moves between devices by JAX's collectives and lax.ppermute only.
A program may use at most 128 MiB of HBM per device.

v0:
```python
import jax
import jax.numpy as jnp
from jax import lax
from jax.experimental import pallas as pl
from jax.experimental.pallas import tpu as pltpu
from jax.sharding import Mesh, PartitionSpec as P

FIX_ONE = 1.0 - 0.9**10
FIX_TWO = 1.0 - 0.95**10
F32 = jnp.float32
BF = jnp.bfloat16
NX, NZ, NC, NM = 4, 8, 2, 4
B = 16
W = 256
PAD = 16


def contract(left, right, left_dim, right_dim):
    return lax.dot_general(
        left, right, (((left_dim,), (right_dim,)), ((), ())), preferred_element_type=F32
    )


def swap_cores(value):
    return lax.ppermute(value, "c", [(0, 1), (1, 0)])


def exchange(value, axis):
    return lax.all_to_all(value, axis, 0, 0, tiled=True)


def everyone(value, axis, count):
    return exchange(jnp.broadcast_to(value[None], (count, *value.shape)), axis)


def ordered(core, mine, other):
    return jnp.where(core == 0, jnp.stack([mine, other]), jnp.stack([other, mine]))


VMEM = pl.BlockSpec(memory_space=pltpu.VMEM)
SMEM = pl.BlockSpec(memory_space=pltpu.SMEM)


def dot_nn(a, b):
    return contract(a, b, 1, 0)


def dot_nt(a, b):
    return contract(a, b, 1, 1)


def dot_tn(a, b):
    return contract(a, b, 0, 0)


def call(kernel, name, outs, scratch, *args):
    n_scalar = 1
    return pl.pallas_call(
        kernel,
        out_shape=[jax.ShapeDtypeStruct(s, d) for s, d in outs],
        in_specs=[SMEM] * n_scalar + [VMEM] * (len(args) - n_scalar),
        out_specs=[VMEM] * len(outs),
        scratch_shapes=[pltpu.VMEM(s, d) for s, d in scratch],
        compiler_params=pltpu.CompilerParams(vmem_limit_bytes=48 * 1024 * 1024),
        name=name,
    )(*args)


def pack_kernel(where, lb, rb, m1, m2, sl, sr, out):
    for k, ref in enumerate((lb, rb, m1, m2, sl, sr)):
        out[:, k] = ref[...].astype(BF)


def block_start(index, size):
    return pl.multiple_of(index * size, size)


def prep_kernel(where, own, oth, left, right):
    c = where[2]

    def step(k, carry):
        z, xp = k // NX, k % NX
        start = xp * (NZ * NC * B) + z * (NC * B)
        for ref, core in ((own, c), (oth, 1 - c)):
            row = pl.multiple_of(start + core * B, B)
            for arr, out in ((0, left), (1, right)):
                for m in range(NM):
                    out[pl.ds(row, B), m * W : (m + 1) * W] = ref[m, z, arr * NX + xp]
        return carry

    lax.fori_loop(0, NZ * NX, step, 0)


def old_power_kernel(where, s0, s1, s2, s3, left, right, out, stats):
    c, m = where[2], where[3]

    def step(k, carry):
        z, xp = k // NX, k % NX
        for core in range(NC):
            row = pl.multiple_of(xp * (NZ * NC * B) + z * (NC * B) + core * B, B)
            for shift, ref in enumerate((s0, s1, s2, s3)):
                col = block_start(lax.rem(m + NM - shift, NM), W)
                stats[pl.ds(row, B), pl.ds(col, W)] = ref[z, core * NX + xp]
        return carry

    lax.fori_loop(0, NZ * NX, step, 0)

    def product(basis):
        def rows(i, carry):
            r = pl.ds(block_start(i, W), W)
            out[r, :] = dot_nn(stats[r, :], basis[...])
            return carry

        lax.fori_loop(0, NM, rows, 0)

    @pl.when(c == 0)
    def _():
        product(left)

    @pl.when(c == 1)
    def _():
        product(right)


def rotate_kernel(where, own, oth, left, right, pack, grad, work, direct, rot_home, rot):
    z, c, m = where[1], where[2], where[3]
    half = own.shape[1]
    for ref, core in ((own, c), (oth, 1 - c)):
        r = pl.ds(block_start(core, half), half)
        for k in range(NM):
            grad[r, k * W : (k + 1) * W] = ref[k]
    col = pl.ds(block_start(m, W), W)

    @pl.when(c == 0)
    def _():
        def rows(i, carry):
            r = pl.ds(block_start(i, W), W)
            work[r, :] = dot_tn(left[:, r], grad[...]).astype(BF)
            rot[r, :] = dot_nn(work[r, :], right[:, col])
            return carry

        lax.fori_loop(0, NM, rows, 0)

    @pl.when(c == 1)
    def _():
        def rows(i, carry):
            r = pl.ds(block_start(i, W), W)
            work[r, :] = dot_nn(grad[r, :], right[...]).astype(BF)
            return carry

        lax.fori_loop(0, NM, rows, 0)

        def more(i, carry):
            r = pl.ds(block_start(i, W), W)
            rot[r, :] = dot_tn(left[:, r], work[:, col])
            return carry

        lax.fori_loop(0, NM, more, 0)

    def step(k, carry):
        xp, zp = k // NZ, k % NZ
        value = rot[pl.ds(pl.multiple_of(k * (NC * B) + c * B, B), B), :]
        one = 0.9 * pack[zp, 2 * NX + xp].astype(F32) + 0.1 * value
        two = 0.95 * pack[zp, 3 * NX + xp].astype(F32) + 0.05 * value * value
        value = (one / FIX_ONE / (jnp.sqrt(two / FIX_TWO) + 1e-08)).astype(BF)
        for copy in range(NM):
            direct[copy, pl.ds(block_start(k, B), B), :] = value
        return carry

    lax.fori_loop(0, NX * NZ, step, 0)
    for xp in range(NX):
        row = pl.multiple_of(xp * (NZ * NC * B) + z * (NC * B) + c * B, B)
        rot_home[xp] = rot[pl.ds(row, B), :].astype(BF)


def power_kernel(where, grad, work, old, outer, basis, power, iterate):
    z, c, m = where[1], where[2], where[3]
    col = pl.ds(block_start(m, W), W)
    total = NM * W

    def z_rows(xp):
        return pl.ds(pl.multiple_of(xp * (NZ * NC * B) + z * (NC * B), NC * B), NC * B)

    @pl.when(c == 0)
    def _():
        def rows(i, sums):
            r = pl.ds(block_start(i, W), W)
            value = 0.95 * old[r, :] + 0.05 * dot_nt(grad[r, :], work[...])
            power[r, :] = value
            return sums + jnp.sum(value * value, axis=0, keepdims=True)

        sums = lax.fori_loop(0, NM, rows, jnp.zeros((1, total), F32))
        scale = lax.rsqrt(sums + 1e-06)
        for i in range(NM):
            r = slice(i * W, (i + 1) * W)
            iterate[r, :] = (power[r, :] * scale).astype(BF)
        for xp in range(NX):
            outer[xp] = dot_nt(grad[z_rows(xp), :], grad[col, :]).astype(BF)

    @pl.when(c == 1)
    def _():
        def rows(i, sums):
            r = pl.ds(block_start(i, W), W)
            value = 0.95 * old[r, :] + 0.05 * dot_tn(grad[:, r], work[...])
            power[r, :] = value
            return sums + jnp.sum(value * value, axis=0, keepdims=True)

        sums = lax.fori_loop(0, NM, rows, jnp.zeros((1, total), F32))
        scale = lax.rsqrt(sums + 1e-06)
        for i in range(NM):
            r = slice(i * W, (i + 1) * W)
            iterate[r, :] = (power[r, :] * scale).astype(BF)

        def gram_rows(i, carry):
            r = pl.ds(block_start(i, W), W)
            power[r, 0:W] = dot_tn(grad[:, r], grad[:, col])
            return carry

        lax.fori_loop(0, NM, gram_rows, 0)
        for xp in range(NX):
            outer[xp] = power[z_rows(xp), 0:W].astype(BF)

    gram = dot_tn(iterate[:, col], iterate[...]).astype(BF)
    for xp in range(NX):
        here = iterate[z_rows(xp), :]
        value = 1.5 * iterate[z_rows(xp), col].astype(F32) - 0.5 * dot_nt(here, gram)
        basis[xp] = value.astype(BF)


def back_kernel(where, direct, right, back):
    m = where[3]
    rows = pl.ds(block_start(m, W), W)
    total = dot_nt(direct[0], right[rows, 0:W])
    for k in range(1, NM):
        total += dot_nt(direct[k], right[rows, k * W : (k + 1) * W])
    back[...] = total.astype(BF)


def update_kernel(where, own, oth, left, rot_home, outer, basis, norm, sent, back):
    c = where[2]
    half = own.shape[0]

    def step(k, carry):
        src = pl.ds(block_start(k, B), B)
        for ref, core in ((own, c), (oth, 1 - c)):
            back[pl.ds(pl.multiple_of(k * (NC * B) + core * B, B), B), :] = ref[src, :]
        return carry

    lax.fori_loop(0, NX * NZ, step, 0)
    value = dot_nn(left[pl.ds(block_start(c, half), half), :], back[...]).astype(BF)
    for xp in range(NX):
        sent[xp, :half] = value
        sent[xp, half : half + B] = rot_home[xp]
        sent[xp, half + B : half + 3 * B] = outer[xp]
        sent[xp, half + 3 * B : half + 5 * B] = basis[xp]
        sent[xp, half + 5 * B :] = norm[...]


def relay_kernel(where, got, own_slot, sent):
    c = where[2]
    half = own_slot.shape[0]

    def owned(hit, tile):
        value = got[tile, :half]
        return jnp.where(hit > 0, value.astype(F32), 0.0).astype(BF)

    own_slot[...] = owned(where[4], where[5])
    sent[:half] = owned(where[6], where[7])
    nb = NX * B
    for t in range(NX):
        row = pl.multiple_of((1 - c) * B, B)
        sent[half + t * B : half + (t + 1) * B] = got[t, pl.ds(half + B + row, B)]
        sent[half + nb + t * B : half + nb + (t + 1) * B] = got[
            t, pl.ds(half + 3 * B + row, B)
        ]
    sent[half + 2 * nb :] = got[0, half + 5 * B :]
    for t in range(NX):
        sent[half + 2 * nb + t : half + 2 * nb + t + 1] = got[t, half + 5 * B : half + 5 * B + 1]


def final_kernel(
    where, got, own_slot, recv, m1, m2, sl, sr, o1, o2, osl, osr, obl, obr, slot
):
    c = where[2]
    half = own_slot.shape[0]
    nb = NX * B
    slot[0, pl.ds(block_start(c, half), half)] = own_slot[...]
    slot[0, pl.ds(block_start(1 - c, half), half)] = recv[:half]
    row = pl.multiple_of(c * B, B)
    for t in range(NX):
        rot = got[t, half : half + B].astype(F32)
        o1[t] = 0.9 * m1[t] + 0.1 * rot
        o2[t] = 0.95 * m2[t] + 0.05 * rot * rot
        outer_own = got[t, pl.ds(half + B + row, B)].astype(F32)
        outer_oth = recv[half + t * B : half + (t + 1) * B].astype(F32)
        basis_own = got[t, pl.ds(half + 3 * B + row, B)].astype(F32)
        basis_oth = recv[half + nb + t * B : half + nb + (t + 1) * B].astype(F32)
        osl[t] = 0.95 * sl[t] + 0.05 * jnp.where(c == 0, outer_own, outer_oth)
        osr[t] = 0.95 * sr[t] + 0.05 * jnp.where(c == 0, outer_oth, outer_own)
        obl[t] = jnp.where(c == 0, basis_own, basis_oth)
        obr[t] = jnp.where(c == 0, basis_oth, basis_own)


def shards(
    features,
    out_grads,
    norm_grads,
    owners,
    moment1,
    moment2,
    left_stats,
    right_stats,
    left_basis,
    right_basis,
    norm_m,
    norm_v,
):
    xi = lax.axis_index("x")
    zi = lax.axis_index("z")
    ci = lax.axis_index("c")
    mi = lax.axis_index("mp")
    mine_dp = (xi * NZ + zi) * NC + ci
    other_dp = (xi * NZ + zi) * NC + (1 - ci)
    left_core = ci == 0
    half = features.shape[1] // 2
    full = 2 * half
    tile_owner = owners[:NX]

    def owned(index):
        hit = tile_owner == index
        which = jnp.sum(jnp.where(hit, jnp.arange(NX, dtype=jnp.int32), 0))
        return [jnp.any(hit).astype(jnp.int32), which]

    where = jnp.stack([xi, zi, ci, mi, *owned(mine_dp), *owned(other_dp)]).astype(jnp.int32)

    with jax.named_scope("state_rows"):
        (home,) = call(
            pack_kernel,
            "pack",
            [((NX, 6, B, W), BF)],
            [],
            where,
            left_basis,
            right_basis,
            moment1,
            moment2,
            left_stats,
            right_stats,
        )
        rows = exchange(home, "x")
        stats_mine = jnp.where(left_core, rows[:, 4], rows[:, 5])
        stats_send = jnp.where(left_core, rows[:, 5], rows[:, 4])
        stats_recv = swap_cores(stats_send)
        stats_rows = ordered(ci, stats_mine, stats_recv)
        pack = jnp.concatenate(
            [rows[:, :4].swapaxes(0, 1).reshape(16, B, W), stats_rows.reshape(8, B, W)], axis=0
        )
        pack = lax.all_gather(pack, "z", axis=0)

    with jax.named_scope("grad_sum"):
        feat_other = lax.dynamic_slice_in_dim(features, (1 - ci) * half, half, 1)
        feat_mine = lax.dynamic_slice_in_dim(features, ci * half, half, 1)
        norm_parts = norm_grads[0].reshape(NX, NZ, NC, 32)

        def partial(feat, core):
            grads = jnp.einsum("ti,tnc->nic", feat, out_grads, preferred_element_type=F32)
            norm = lax.dynamic_index_in_dim(norm_parts, core, 2, keepdims=False)
            norm = jnp.pad(norm.reshape(NX, 1, W), ((0, 0), (0, PAD - 1), (0, 0)))
            return grads, norm

        grads_o, norm_o = partial(feat_other, 1 - ci)
        sent = jnp.concatenate([grads_o.astype(BF), norm_o.astype(BF)], axis=1)
        got = swap_cores(sent)
        grads_s, norm_s = partial(feat_mine, ci)
        acc = jnp.concatenate([grads_s, norm_s], axis=1) + got.astype(F32)
        acc = exchange(acc.astype(BF), "x")
        acc, pack = lax.optimization_barrier((acc, pack))

    with jax.named_scope("state_all"):
        bases = lax.all_gather(pack[:, :8], "mp", axis=0)
        stats = pack[:, 16:]
        stats_all = [stats] + [
            lax.ppermute(stats, "mp", [(i, (i + s) % NM) for i in range(NM)]) for s in (1, 2, 3)
        ]
        bases_other = swap_cores(bases)
        left, right = call(
            prep_kernel, "prep", [((full, full), BF)] * 2, [], where, bases, bases_other
        )
        (power_old,) = call(
            old_power_kernel,
            "old_power",
            [((full, full), F32)],
            [((full, full), BF)],
            where,
            *stats_all,
            left,
            right,
        )

    with jax.named_scope("grad_sum"):
        acc = jnp.sum(acc.astype(F32), axis=0)
        norm_z = jnp.pad(acc[half].reshape(NZ, 1, 32), ((0, 0), (0, PAD - 1), (0, W - 32)))
        acc = jnp.concatenate([acc[:half].reshape(NZ, half // NZ, W), norm_z], axis=1)
        acc = exchange(acc.astype(BF), "z")
        acc = jnp.sum(acc.astype(F32), axis=0)
        grad_rows = acc[: half // NZ].astype(BF)
        norm_total = acc[half // NZ, :32]

    new_nm = 0.9 * norm_m + 0.1 * norm_total
    new_nv = 0.95 * norm_v + 0.05 * norm_total * norm_total
    norm_step = new_nm / FIX_ONE / (jnp.sqrt(new_nv / FIX_TWO) + 1e-08)

    with jax.named_scope("grad_all"):
        norm_row = jnp.pad(norm_step.astype(BF)[None], ((0, PAD - 1), (0, W - 32)))
        grad_z = everyone(jnp.concatenate([grad_rows, norm_row], axis=0), "z", NZ)
        norm_zs = grad_z[:, half // NZ, :32].reshape(1, W)
        grad_half = grad_z[:, : half // NZ].reshape(half, W)
        grad_half = everyone(grad_half, "mp", NM)
        grad_other = swap_cores(grad_half)

    with jax.named_scope("rotate"):
        grad, work, direction, rot_home = call(
            rotate_kernel,
            "rotate",
            [
                ((full, full), BF),
                ((full, full), BF),
                ((NM, half, W), BF),
                ((NX, B, W), BF),
            ],
            [((full, W), F32)],
            where,
            grad_half,
            grad_other,
            left,
            right,
            pack,
        )
        direction = exchange(direction, "mp")
    with jax.named_scope("power"):
        outer, basis = call(
            power_kernel,
            "power",
            [((NX, NC * B, W), BF)] * 2,
            [((full, full), F32), ((full, full), BF)],
            where,
            grad,
            work,
            power_old,
        )
    with jax.named_scope("update"):
        (back,) = call(back_kernel, "back", [((half, W), BF)], [], where, direction, right)
        back_other = swap_cores(back)
        norm_pad = jnp.pad(norm_zs, ((0, PAD - 1), (0, 0)))
        (sent,) = call(
            update_kernel,
            "update",
            [((NX, half + 5 * B + PAD, W), BF)],
            [((full, W), BF)],
            where,
            back,
            back_other,
            left,
            rot_home,
            outer,
            basis,
            norm_pad,
        )

    with jax.named_scope("home"):
        got = exchange(sent, "x")
        nb = NX * B
        own_slot, sent = call(
            relay_kernel,
            "relay",
            [((half, W), BF), ((half + 2 * nb + PAD, W), BF)],
            [],
            where,
            got,
        )
        recv = swap_cores(sent)
        state = ((NX, B, W), F32)
        outs = call(
            final_kernel,
            "final",
            [state] * 6 + [((1, full, W), BF)],
            [],
            where,
            got,
            own_slot,
            recv,
            moment1,
            moment2,
            left_stats,
            right_stats,
        )
        norm_xz = got[:, half + 5 * B]
        norm_all = ordered(ci, norm_xz, recv[half + 2 * nb : half + 2 * nb + NX])
        norm_all = norm_all.reshape(NC, NX, NZ, 32).transpose(1, 2, 0, 3).reshape(1, -1)
        norm_slot = jnp.where(mine_dp == owners[NX], norm_all.astype(F32), 0.0)
    return (*outs, new_nm, new_nv, norm_slot)


def solution(mesh):
    mesh = Mesh(mesh.devices.reshape(NX, NZ, NC, NM), ("x", "z", "c", "mp"))
    dp = ("x", "z", "c")
    state = P(None, dp, "mp")
    in_specs = (
        P(dp, None),
        P(dp, None, "mp"),
        P(dp, None),
        P(),
        state,
        state,
        state,
        state,
        state,
        state,
        P(dp),
        P(dp),
    )
    out_specs = (
        state,
        state,
        state,
        state,
        state,
        state,
        P(dp, None, "mp"),
        P(dp),
        P(dp),
        P(dp, None),
    )
    return jax.shard_map(shards, mesh=mesh, in_specs=in_specs, out_specs=out_specs, check_vma=False)
```

profile of v0, /device:TPU:1, one launch (start us, length us, event | category | flops | bytes accessed | tf_op | source)
XLA Modules:
  0.0 247.1 jit_solution(4478905333618793392)
XLA Ops:
  7.2 1.4 compare_reduce_fusion
  8.7 1.3 fusion.31
  11.2 1.4 stack.67.where
  12.6 0.8 copy-done.13
  13.5 0.8 copy-done.15
  14.3 0.8 copy-done.17
  15.2 0.8 copy-done.19
  16.0 0.8 copy-done.21
  16.8 0.8 copy-done.22
  17.7 1.2 pack.1
  18.9 4.8 %all-to-all-start.1 = ((bf16[4,6,16,256]{3,2,1,0:T(8,128)(2,1)}), bf16[4,6,16,256]{3,2,1,0:T(8,128)(2,1)S(1)}, u32[]{:S(2)}, u32[]{:S(2)}) async-start(bf16[4,6,16,256]{3,2,1,0:T(8,128)(2,1)} %pack.1), calls=%async_computation.1 | async-start | bytes 393216 | tf_op jit(solution)/shard_map/state_rows/all_to_all | solution.py:29
  24.3 1.4 reduce.10
  25.7 3.2 %all-to-all-done.1 = bf16[4,6,16,256]{3,2,1,0:T(8,128)(2,1)S(1)} async-done(((bf16[4,6,16,256]{3,2,1,0:T(8,128)(2,1)}), bf16[4,6,16,256]{3,2,1,0:T(8,128)(2,1)S(1)}, u32[]{:S(2)}, u32[]{:S(2)}) %all-to-all-start.1) | async-done | bytes 196640 | tf_op jit(solution)/shard_map/state_rows/all_to_all | solution.py:29
  28.9 3.0 %collective-permute-start.1 = (bf16[4,16,256]{2,1,0:T(8,128)(2,1)S(1)}, bf16[4,16,256]{2,1,0:T(8,128)(2,1)S(1)}, u32[]{:S(2)}, u32[]{:S(2)}) collective-permute-start(bf16[4,16,256]{2,1,0:T(8,128)(2,1)S(1)} %fusion.25), channel_id=1, source_target_pairs={{0,4},{4,0},{1,5},{5,1},{2,6},{6,2},{3,7},{7,3},{8,12},{12,8},{9,1... | collective-permute-start | bytes 98312 | tf_op jit(solution)/shard_map/state_rows/ppermute | solution.py:25
  32.0 0.8 collective-permute-done.1
  32.8 0.7 pad_maximum_fusion
  33.7 2.5 %fusion.13 = bf16[4,512,256]{2,1,0:T(8,128)(2,1)S(1)} fusion(bf16[1024,4,256]{2,1,0:T(4,128)(2,1)S(1)} %copy-done, bf16[1024,1024]{1,0:T(8,128)(2,1)} %param.12, s32[]{:T(128)S(6)} %select_n.92), kind=kOutput, calls=%fused_computation.11 | convolution fusion | flops 1074266112 | bytes 4194308 | tf_op jit(solution)/shard_map/grad_sum/ti,tnc->nic/dot_general | solution.py:366
  36.2 1.1 fusion.16
  37.7 2.5 %fusion.7 = f32[4,512,256]{2,1,0:T(8,128)S(1)} fusion(bf16[1024,4,256]{2,1,0:T(4,128)(2,1)S(1)} %copy-done, bf16[1024,1024]{1,0:T(8,128)(2,1)} %param.12, s32[]{:T(128)S(6)} %select_n.90), kind=kOutput, calls=%fused_computation.9 | convolution fusion | flops 1073741824 | bytes 5242884 | tf_op jit(solution)/shard_map/grad_sum/ti,tnc->nic/dot_general | solution.py:366
  40.5 17.4 %all_to_all.35 = bf16[4,528,256]{2,1,0:T(8,128)(2,1)S(1)} all-to-all(bf16[4,528,256]{2,1,0:T(8,128)(2,1)S(1)} %fusion.1), channel_id=1, replica_groups=mesh['x'=4,'z'=8,'c'=2,'mp'=4] {'x'}, dimensions={0} | all-to-all | bytes 2162688 | tf_op jit(solution)/shard_map/grad_sum/all_to_all | solution.py:29
  58.0 11.9 %all-gather.5.cloned.1.call-done = bf16[192,16,256]{2,1,0:T(8,128)(2,1)} async-done(((bf16[24,16,256]{2,1,0:T(8,128)(2,1)}), bf16[192,16,256]{2,1,0:T(8,128)(2,1)}) %all-gather.5.cloned.1.call-update) | async-done | bytes 1572880 | tf_op jit(solution)/shard_map/state_rows/all_gather | solution.py:358
  69.9 2.3 fusion.33
  72.6 13.4 %all_to_all.36 = bf16[8,80,256]{2,1,0:T(8,128)(2,1)S(1)} all-to-all(bf16[8,80,256]{2,1,0:T(8,128)(2,1)S(1)} %fusion.22), channel_id=1, replica_groups=mesh['x'=4,'z'=8,'c'=2,'mp'=4] {'z'}, dimensions={0} | all-to-all | bytes 655360 | tf_op jit(solution)/shard_map/grad_sum/all_to_all | solution.py:29
  86.6 0.8 broadcast_in_dim.27
  87.4 3.4 %all-to-all-start.3 = ((bf16[8,80,256]{2,1,0:T(8,128)(2,1)}), bf16[8,80,256]{2,1,0:T(8,128)(2,1)S(1)}, u32[]{:S(2)}, u32[]{:S(2)}) async-start(bf16[8,80,256]{2,1,0:T(8,128)(2,1)} %broadcast_in_dim.27), calls=%async_computation.3 | async-start | bytes 655360 | tf_op jit(solution)/shard_map/grad_all/all_to_all | solution.py:29
  90.8 17.3 %all-gather.7.cloned.1.call-done = bf16[32,8,16,256]{3,2,1,0:T(8,128)(2,1)} async-done(((bf16[8,8,16,256]{3,2,1,0:T(8,128)(2,1)}), bf16[32,8,16,256]{3,2,1,0:T(8,128)(2,1)}) %all-gather.7.cloned.1.call-update) | async-done | bytes 2097168 | tf_op jit(solution)/shard_map/state_all/all_gather | solution.py:380
  108.1 0.7 collective-permute-start.3
  108.9 16.6 %all_to_all.37.own = bf16[4,512,256]{2,1,0:T(8,128)(2,1)S(1)} all-to-all(bf16[4,512,256]{2,1,0:T(8,128)(2,1)S(1)} %broadcast_in_dim.29), channel_id=1, replica_groups=mesh['x'=4,'z'=8,'c'=2,'mp'=4] {'mp'}, dimensions={0} | all-to-all | bytes 2097152 | tf_op jit(solution)/shard_map/grad_all/all_to_all | solution.py:29
  125.5 2.0 collective-permute-start.2
  127.5 2.8 %prep.1 = (bf16[1024,1024]{1,0:T(8,128)(2,1)S(1)}, bf16[1024,1024]{1,0:T(8,128)(2,1)S(1)}) custom-call(s32[8]{0:T(128)S(1)} %stack.67.where, bf16[4,8,8,16,256]{4,3,2,1,0:T(8,128)(2,1)} %bitcast.71, bf16[4,8,8,16,256]{4,3,2,1,0:T(8,128)(2,1)} %collective-permute-done.3.oth), custom_call_target="tpu_custom_call" | custom-call | tf_op jit(solution)/shard_map/state_all/prep/pallas_call | solution.py:58
  130.3 1.3 copy-done.1
  131.7 1.3 copy-done.4
  133.0 10.0 %rotate.1 = (bf16[1024,1024]{1,0:T(8,128)(2,1)}, bf16[1024,1024]{1,0:T(8,128)(2,1)}, bf16[4,512,256]{2,1,0:T(8,128)(2,1)S(1)}, bf16[4,16,256]{2,1,0:T(8,128)(2,1)S(1)}) custom-call(s32[8]{0:T(128)S(1)} %stack.67.where, bf16[4,512,256]{2,1,0:T(8,128)(2,1)S(1)} %all_to_all.37.own, bf16[4,512,256]{2,1,0:T(8,128)(2,1)S(1)} %collective-permute-done.2.oth, ...), custom_call_target="tpu_custom_call" | custom-call | tf_op jit(solution)/shard_map/rotate/rotate/pallas_call | solution.py:58
  143.1 1.0 copy-done.10
  144.1 3.5 %all-to-all-start.5 = ((bf16[4,512,256]{2,1,0:T(8,128)(2,1)}), bf16[4,512,256]{2,1,0:T(8,128)(2,1)S(1)}, u32[]{:S(2)}, u32[]{:S(2)}) async-start(bf16[4,512,256]{2,1,0:T(8,128)(2,1)} %copy-done.10), calls=%async_computation.5 | async-start | bytes 2097152 | tf_op jit(solution)/shard_map/rotate/all_to_all | solution.py:29
  147.6 2.6 %collective-permute-start.7 = (bf16[8,8,16,256]{3,2,1,0:T(8,128)(2,1)}, bf16[8,8,16,256]{3,2,1,0:T(8,128)(2,1)}, u32[]{:S(2)}, u32[]{:S(2)}) collective-permute-start(bf16[8,8,16,256]{3,2,1,0:T(8,128)(2,1)} %get-tuple-element.55.s0), channel_id=1, source_target_pairs={{0,3},{1,0},{2,1},{3,2},{4,7},{5,4},{6,5},{7,6},{8,11},{9,8},{10,9... | collective-permute-start | bytes 1572872 | tf_op jit(solution)/shard_map/state_all/ppermute | solution.py:383
  150.3 0.6 collective-permute-start.6
  150.8 0.6 collective-permute-start.5
  151.4 11.8 %all-to-all-done.5.direct = bf16[4,512,256]{2,1,0:T(8,128)(2,1)S(1)} async-done(((bf16[4,512,256]{2,1,0:T(8,128)(2,1)}), bf16[4,512,256]{2,1,0:T(8,128)(2,1)S(1)}, u32[]{:S(2)}, u32[]{:S(2)}) %all-to-all-start.5) | async-done | bytes 1048608 | tf_op jit(solution)/shard_map/rotate/all_to_all | solution.py:29
  163.2 1.6 copy-done.5
  164.8 1.0 back.1.own
  165.8 0.7 collective-permute-start.4
  166.5 0.7 slice_reduce_fusion.1
  167.3 5.7 %collective-permute-done.7.s3 = bf16[8,8,16,256]{3,2,1,0:T(8,128)(2,1)} collective-permute-done((bf16[8,8,16,256]{3,2,1,0:T(8,128)(2,1)}, bf16[8,8,16,256]{3,2,1,0:T(8,128)(2,1)}, u32[]{:S(2)}, u32[]{:S(2)}) %collective-permute-start.7) | collective-permute-done | bytes 524320 | tf_op jit(solution)/shard_map/state_all/ppermute | solution.py:383
  173.0 1.5 collective-permute-done.6.s2
  174.6 10.9 %collective-permute-done.5.s1 = bf16[8,8,16,256]{3,2,1,0:T(8,128)(2,1)} collective-permute-done((bf16[8,8,16,256]{3,2,1,0:T(8,128)(2,1)}, bf16[8,8,16,256]{3,2,1,0:T(8,128)(2,1)}, u32[]{:S(2)}, u32[]{:S(2)}) %collective-permute-start.5) | collective-permute-done | bytes 524320 | tf_op jit(solution)/shard_map/state_all/ppermute | solution.py:383
  185.5 1.6 copy-done.2
  187.0 1.0 copy-done.9
  188.1 8.2 %old_power.1.old = f32[1024,1024]{1,0:T(8,128)} custom-call(s32[8]{0:T(128)S(1)} %stack.67.where, bf16[8,8,16,256]{3,2,1,0:T(8,128)(2,1)S(1)} %copy-done.9, bf16[8,8,16,256]{3,2,1,0:T(8,128)(2,1)} %collective-permute-done.5.s1, bf16[8,8,16,256]{3,2,1,0:T(8,128)(2,1)} %collective-permute-done.6.s2, bf16[8,8,16,256]{3,2,1,0:T(8,128)(2,1)} %collective-permute-done.7.s3, ...), custom_call_target="tpu_custom_call" | custom-call | tf_op jit(solution)/shard_map/state_all/old_power/pallas_call | solution.py:58
  196.3 8.8 %power.1 = (bf16[4,32,256]{2,1,0:T(8,128)(2,1)S(1)}, bf16[4,32,256]{2,1,0:T(8,128)(2,1)S(1)}) custom-call(s32[8]{0:T(128)S(1)} %stack.67.where, bf16[1024,1024]{1,0:T(8,128)(2,1)S(1)} %copy-done.7, bf16[1024,1024]{1,0:T(8,128)(2,1)S(1)} %copy-done.8, f32[1024,1024]{1,0:T(8,128)} %old_power.1.old), custom_call_target="tpu_custom_call" | custom-call | tf_op jit(solution)/shard_map/power/power/pallas_call | solution.py:58
  205.1 1.2 update.1
  206.5 21.3 %all_to_all.38.got = bf16[4,608,256]{2,1,0:T(8,128)(2,1)S(1)} all-to-all(bf16[4,608,256]{2,1,0:T(8,128)(2,1)S(1)} %update.1), channel_id=1, replica_groups=mesh['x'=4,'z'=8,'c'=2,'mp'=4] {'x'}, dimensions={0} | all-to-all | bytes 2490368 | tf_op jit(solution)/shard_map/home/all_to_all | solution.py:29
  227.8 1.4 relay.1
  229.2 0.7 copy-done.11
  229.9 0.8 collective-permute-start.8
  230.6 0.6 slice.62
  232.3 0.7 slice.75
  232.9 0.7 stack.72
  233.6 0.8 select_bitcast_fusion
  234.4 0.6 copy.101
  235.0 1.5 select_n.107
  236.5 0.9 copy-done.12
  237.5 0.8 copy-done.20
  238.3 2.0 final.1
  (77 shorter events, 3.3 us)
Async XLA Ops:
  7.2 26.5 %copy-start = (bf16[1024,4,256]{2,1,0:T(4,128)(2,1)S(1)}, bf16[1024,4,256]{2,1,0:T(4,128)(2,1)}, u32[]{:S(2)}) copy-start(bf16[1024,4,256]{2,1,0:T(4,128)(2,1)} %param.13) | copy-start | bytes 6291460
  12.6 0.8 copy-start.13
  13.5 0.8 copy-start.15
  14.3 0.8 copy-start.17
  15.2 0.8 copy-start.19
  16.0 0.8 copy-start.21
  16.8 0.8 copy-start.22
  18.9 10.0 %all-to-all-start.1 = ((bf16[4,6,16,256]{3,2,1,0:T(8,128)(2,1)}), bf16[4,6,16,256]{3,2,1,0:T(8,128)(2,1)S(1)}, u32[]{:S(2)}, u32[]{:S(2)}) async-start(bf16[4,6,16,256]{3,2,1,0:T(8,128)(2,1)} %pack.1), calls=%async_computation.1 | async-start | bytes 393216 | tf_op jit(solution)/shard_map/state_rows/all_to_all | solution.py:29
  23.8 46.1 %all-gather.5.cloned.1.call-start = ((), (), s32[]{:S(2)}) async-start(), calls=%async_computation.7 | async-start | bytes 1769472 | tf_op jit(solution)/shard_map/state_rows/all_gather | solution.py:358
  28.9 3.8 %collective-permute-start.1 = (bf16[4,16,256]{2,1,0:T(8,128)(2,1)S(1)}, bf16[4,16,256]{2,1,0:T(8,128)(2,1)S(1)}, u32[]{:S(2)}, u32[]{:S(2)}) collective-permute-start(bf16[4,16,256]{2,1,0:T(8,128)(2,1)S(1)} %fusion.25), channel_id=1, source_target_pairs={{0,4},{4,0},{1,5},{5,1},{2,6},{6,2},{3,7},{7,3},{8,12},{12,8},{9,1... | collective-permute-start | bytes 98312 | tf_op jit(solution)/shard_map/state_rows/ppermute | solution.py:25
  33.5 74.6 %all-gather.7.cloned.1.call-start = ((), (), s32[]{:S(2)}) async-start(), calls=%async_computation.8 | async-start | bytes 2621440 | tf_op jit(solution)/shard_map/state_all/all_gather | solution.py:380
  37.3 2.9 %collective-permute-start = (bf16[4,528,256]{2,1,0:T(8,128)(2,1)}, bf16[4,528,256]{2,1,0:T(8,128)(2,1)S(1)}, u32[]{:S(2)}, u32[]{:S(2)}) collective-permute-start(bf16[4,528,256]{2,1,0:T(8,128)(2,1)} %fusion.16), channel_id=1, source_target_pairs={{0,4},{4,0},{1,5},{5,1},{2,6},{6,2},{3,7},{7,3},{8,12},{12,8},{9,1... | collective-permute-start | bytes 3244040 | tf_op jit(solution)/shard_map/grad_sum/ppermute | solution.py:25
  72.1 13.9 %copy-start.25 = (f32[32]{0:T(128)S(1)}, f32[32]{0:T(128)}, u32[]{:S(2)}) copy-start(f32[32]{0:T(128)} %param.22) | copy-start | bytes 388
  72.1 13.9 %copy-start.26 = (f32[32]{0:T(128)S(1)}, f32[32]{0:T(128)}, u32[]{:S(2)}) copy-start(f32[32]{0:T(128)} %param.23) | copy-start | bytes 388
  87.4 21.4 %all-to-all-start.3 = ((bf16[8,80,256]{2,1,0:T(8,128)(2,1)}), bf16[8,80,256]{2,1,0:T(8,128)(2,1)S(1)}, u32[]{:S(2)}, u32[]{:S(2)}) async-start(bf16[8,80,256]{2,1,0:T(8,128)(2,1)} %broadcast_in_dim.27), calls=%async_computation.3 | async-start | bytes 655360 | tf_op jit(solution)/shard_map/grad_all/all_to_all | solution.py:29
  108.1 19.4 %collective-permute-start.3 = (bf16[4,8,8,16,256]{4,3,2,1,0:T(8,128)(2,1)}, bf16[4,8,8,16,256]{4,3,2,1,0:T(8,128)(2,1)}, u32[]{:S(2)}, u32[]{:S(2)}) collective-permute-start(bf16[4,8,8,16,256]{4,3,2,1,0:T(8,128)(2,1)} %bitcast.70), channel_id=1, source_target_pairs={{0,4},{4,0},{1,5},{5,1},{2,6},{6,2},{3,7},{7,3},{8,12},{12,8},{9,1... | collective-permute-start | bytes 6291464 | tf_op jit(solution)/shard_map/state_all/ppermute | solution.py:25
  108.8 21.5 %copy-start.23 = (bf16[8,80,256]{2,1,0:T(8,128)(2,1)}, bf16[8,80,256]{2,1,0:T(8,128)(2,1)S(1)}, u32[]{:S(2)}) copy-start(bf16[8,80,256]{2,1,0:T(8,128)(2,1)S(1)} %all-to-all-done.3) | copy-start | bytes 983044
  125.5 7.6 %copy-start.6 = (bf16[192,16,256]{2,1,0:T(8,128)(2,1)S(1)}, bf16[192,16,256]{2,1,0:T(8,128)(2,1)}, u32[]{:S(2)}) copy-start(bf16[192,16,256]{2,1,0:T(8,128)(2,1)} %all-gather.5.cloned.1.call-done) | copy-start | bytes 4718596
  125.5 7.5 %collective-permute-start.2 = (bf16[4,512,256]{2,1,0:T(8,128)(2,1)S(1)}, bf16[4,512,256]{2,1,0:T(8,128)(2,1)S(1)}, u32[]{:S(2)}, u32[]{:S(2)}) collective-permute-start(bf16[4,512,256]{2,1,0:T(8,128)(2,1)S(1)} %all_to_all.37.own), channel_id=1, source_target_pairs={{0,4},{4,0},{1,5},{5,1},{2,6},{6,2},{3,7},{7,3},{8,12},{12,8},{9,1... | collective-permute-start | bytes 3145736 | tf_op jit(solution)/shard_map/grad_all/ppermute | solution.py:25
  130.3 1.4 copy-start.1
  131.7 1.3 copy-start.4
  143.1 1.0 copy-start.10
  144.1 19.1 %all-to-all-start.5 = ((bf16[4,512,256]{2,1,0:T(8,128)(2,1)}), bf16[4,512,256]{2,1,0:T(8,128)(2,1)S(1)}, u32[]{:S(2)}, u32[]{:S(2)}) async-start(bf16[4,512,256]{2,1,0:T(8,128)(2,1)} %copy-done.10), calls=%async_computation.5 | async-start | bytes 2097152 | tf_op jit(solution)/shard_map/rotate/all_to_all | solution.py:29
  147.6 25.4 %collective-permute-start.7 = (bf16[8,8,16,256]{3,2,1,0:T(8,128)(2,1)}, bf16[8,8,16,256]{3,2,1,0:T(8,128)(2,1)}, u32[]{:S(2)}, u32[]{:S(2)}) collective-permute-start(bf16[8,8,16,256]{3,2,1,0:T(8,128)(2,1)} %get-tuple-element.55.s0), channel_id=1, source_target_pairs={{0,3},{1,0},{2,1},{3,2},{4,7},{5,4},{6,5},{7,6},{8,11},{9,8},{10,9... | collective-permute-start | bytes 1572872 | tf_op jit(solution)/shard_map/state_all/ppermute | solution.py:383
  150.3 24.3 %collective-permute-start.6 = (bf16[8,8,16,256]{3,2,1,0:T(8,128)(2,1)}, bf16[8,8,16,256]{3,2,1,0:T(8,128)(2,1)}, u32[]{:S(2)}, u32[]{:S(2)}) collective-permute-start(bf16[8,8,16,256]{3,2,1,0:T(8,128)(2,1)} %get-tuple-element.55.s0), channel_id=1, source_target_pairs={{0,2},{1,3},{2,0},{3,1},{4,6},{5,7},{6,4},{7,5},{8,10},{9,11},{10,... | collective-permute-start | bytes 1572872 | tf_op jit(solution)/shard_map/state_all/ppermute | solution.py:383
  150.8 34.6 %collective-permute-start.5 = (bf16[8,8,16,256]{3,2,1,0:T(8,128)(2,1)}, bf16[8,8,16,256]{3,2,1,0:T(8,128)(2,1)}, u32[]{:S(2)}, u32[]{:S(2)}) collective-permute-start(bf16[8,8,16,256]{3,2,1,0:T(8,128)(2,1)} %get-tuple-element.55.s0), channel_id=1, source_target_pairs={{0,1},{1,2},{2,3},{3,0},{4,5},{5,6},{6,7},{7,4},{8,9},{9,10},{10,1... | collective-permute-start | bytes 1572872 | tf_op jit(solution)/shard_map/state_all/ppermute | solution.py:383
  163.2 1.6 copy-start.5
  165.8 39.3 %collective-permute-start.4 = (bf16[512,256]{1,0:T(8,128)(2,1)S(1)}, bf16[512,256]{1,0:T(8,128)(2,1)S(1)}, u32[]{:S(2)}, u32[]{:S(2)}) collective-permute-start(bf16[512,256]{1,0:T(8,128)(2,1)S(1)} %back.1.own), channel_id=1, source_target_pairs={{0,4},{4,0},{1,5},{5,1},{2,6},{6,2},{3,7},{7,3},{8,12},{12,8},{9,1... | collective-permute-start | bytes 786440 | tf_op jit(solution)/shard_map/update/ppermute | solution.py:25
  185.5 1.6 copy-start.2
  187.0 1.0 copy-start.9
  188.1 8.2 %copy-start.7 = (bf16[1024,1024]{1,0:T(8,128)(2,1)S(1)}, bf16[1024,1024]{1,0:T(8,128)(2,1)}, u32[]{:S(2)}) copy-start(bf16[1024,1024]{1,0:T(8,128)(2,1)} %get-tuple-element.35.grad) | copy-start | bytes 6291460
  188.1 8.2 %copy-start.8 = (bf16[1024,1024]{1,0:T(8,128)(2,1)S(1)}, bf16[1024,1024]{1,0:T(8,128)(2,1)}, u32[]{:S(2)}) copy-start(bf16[1024,1024]{1,0:T(8,128)(2,1)} %get-tuple-element.36.work) | copy-start | bytes 6291460
  196.3 8.8 %copy-start.3 = (bf16[1024,1024]{1,0:T(8,128)(2,1)S(1)}, bf16[1024,1024]{1,0:T(8,128)(2,1)}, u32[]{:S(2)}) copy-start(bf16[1024,1024]{1,0:T(8,128)(2,1)} %copy-done.1) | copy-start | bytes 6291460
  206.4 24.2 %copy-start.24 = (s32[5]{0:T(128)S(1)}, s32[5]{0:T(128)}, u32[]{:S(2)}) copy-start(s32[5]{0:T(128)} %param.15) | copy-start | bytes 64
  206.4 30.1 %copy-start.14 = (f32[4,16,256]{2,1,0:T(8,128)S(1)}, f32[4,16,256]{2,1,0:T(8,128)}, u32[]{:S(2)}) copy-start(f32[4,16,256]{2,1,0:T(8,128)} %m1.3) | copy-start | bytes 196612
  206.4 30.1 %copy-start.16 = (f32[4,16,256]{2,1,0:T(8,128)S(1)}, f32[4,16,256]{2,1,0:T(8,128)}, u32[]{:S(2)}) copy-start(f32[4,16,256]{2,1,0:T(8,128)} %m2.3) | copy-start | bytes 196612
  206.4 30.1 %copy-start.18 = (f32[4,16,256]{2,1,0:T(8,128)S(1)}, f32[4,16,256]{2,1,0:T(8,128)}, u32[]{:S(2)}) copy-start(f32[4,16,256]{2,1,0:T(8,128)} %sl.3) | copy-start | bytes 196612
  229.2 0.7 copy-start.11
  229.9 2.4 collective-permute-start.8
  236.5 1.0 copy-start.12
  237.5 0.8 copy-start.20
Sparse Core Ops, SparseCore 0:
  33.6 36.2 all-gather.4
  72.3 35.7 all-gather.6
where the time goes:
time: 249 us; the launch traced here: 247 us
  blocking collectives  68.7 us (28%)
  waiting for transfers between devices  63.5 us (26%)
  Pallas kernels  36.8 us (15%)
  local copies, waits for them, and re-layouts  25.9 us (10%)
  starting transfers between devices  23 us (9%)
  between operations  16.3 us (7%)
  other arithmetic  7.91 us (3%)
  matrix products  4.99 us (2%)
    all_to_all x4, blocking collectives, exchange(): return lax.all_to_all(value, axis, 0, 0, tiled=True)  68.7 us
    pallas_call x9, Pallas kernels, call(): pl.pallas_call(kernel, out_shape=[jax.ShapeDtypeStruct(s, d) for s, d in...  36.8 us
    ppermute x3, waiting for transfers between devices, shards(): lax.ppermute(stats, 'mp', [(i, (i + s) % NM) for i in range(NM)])  18.1 us
    all_gather x1, waiting for transfers between devices, shards(): bases = lax.all_gather(pack[:, :8], 'mp', axis=0)  17.3 us
    unnamed x55, local copies, waits for them, and re-layouts  16 us
    all_to_all x3, waiting for transfers between devices, exchange(): return lax.all_to_all(value, axis, 0, 0, tiled=True)  15 us
    all_gather x1, waiting for transfers between devices, shards(): pack = lax.all_gather(pack, 'z', axis=0)  11.9 us
    all_to_all x3, starting transfers between devices, exchange(): return lax.all_to_all(value, axis, 0, 0, tiled=True)  11.8 us
  transfers between devices with their start and end apart: 14, of which 9 were waited for; matrix products, arithmetic and copies ran while one was open for 5% of the time, Pallas kernels for 8%

commit v1 on v0

--- a/solution.py
+++ b/solution.py
@@ -41,6 +41,9 @@
 SMEM = pl.BlockSpec(memory_space=pltpu.SMEM)
 
 
+COST = pl.CostEstimate(flops=6 * 10**9, bytes_accessed=24 * 10**6, transcendentals=0)
+
+
 def dot_nn(a, b):
     return contract(a, b, 1, 0)
 
@@ -53,7 +56,7 @@
     return contract(a, b, 0, 0)
 
 
-def call(kernel, name, outs, scratch, *args):
+def call(kernel, name, outs, scratch, *args, cost=None):
     n_scalar = 1
     return pl.pallas_call(
         kernel,
@@ -62,13 +65,40 @@
         out_specs=[VMEM] * len(outs),
         scratch_shapes=[pltpu.VMEM(s, d) for s, d in scratch],
         compiler_params=pltpu.CompilerParams(vmem_limit_bytes=48 * 1024 * 1024),
+        cost_estimate=cost,
         name=name,
     )(*args)
 
 
-def pack_kernel(where, lb, rb, m1, m2, sl, sr, out):
-    for k, ref in enumerate((lb, rb, m1, m2, sl, sr)):
-        out[:, k] = ref[...].astype(BF)
+def pack_kernel(*refs):
+    states, outs, (held, sems) = refs[:6], refs[6:10], refs[10:]
+    x, c = lax.axis_index("x"), lax.axis_index("c")
+    copies = [pltpu.make_async_copy(ref, held.at[k], sems.at[k]) for k, ref in enumerate(states)]
+    for copy in copies:
+        copy.start()
+    for copy in copies:
+        copy.wait()
+    for shift, out in enumerate(outs):
+        tile = lax.rem(x + shift, NX)
+        for k in range(4):
+            out[k] = held[k, tile].astype(BF)
+        lefts, rights = held[4, tile], held[5, tile]
+        out[4] = jnp.where(c == 0, lefts, rights).astype(BF)
+        out[5] = jnp.where(c == 0, rights, lefts).astype(BF)
+
+
+def shift_of(where, xp):
+    return lax.rem(where[0] - xp + NX, NX)
+
+
+def select_kernel(where, pack, bases, near, far):
+    m = where[3]
+    bases[...] = pack[:, 0:8]
+    for out, steps in ((near, (0, 1)), (far, (0, 2))):
+        for j, step in enumerate(steps):
+            shift = shift_of(where, lax.rem(m + step, NM))
+            for core in range(NC):
+                out[:, 2 * core + j] = pack[:, 16 + NX * core + shift]
 
 
 def block_start(index, size):
@@ -79,39 +109,50 @@
     c = where[2]
 
     def step(k, carry):
-        z, xp = k // NX, k % NX
+        z, shift = k // NX, k % NX
+        xp = shift_of(where, shift)
         start = xp * (NZ * NC * B) + z * (NC * B)
         for ref, core in ((own, c), (oth, 1 - c)):
             row = pl.multiple_of(start + core * B, B)
             for arr, out in ((0, left), (1, right)):
                 for m in range(NM):
-                    out[pl.ds(row, B), m * W : (m + 1) * W] = ref[m, z, arr * NX + xp]
+                    out[pl.ds(row, B), m * W : (m + 1) * W] = ref[m, z, arr * NX + shift]
         return carry
 
     lax.fori_loop(0, NZ * NX, step, 0)
 
 
-def old_power_kernel(where, s0, s1, s2, s3, left, right, out, stats):
+def old_power_kernel(where, pack, from1, from3, from2, left, right, out, block):
     c, m = where[2], where[3]
 
-    def step(k, carry):
-        z, xp = k // NX, k % NX
-        for core in range(NC):
-            row = pl.multiple_of(xp * (NZ * NC * B) + z * (NC * B) + core * B, B)
-            for shift, ref in enumerate((s0, s1, s2, s3)):
-                col = block_start(lax.rem(m + NM - shift, NM), W)
-                stats[pl.ds(row, B), pl.ds(col, W)] = ref[z, core * NX + xp]
-        return carry
-
-    lax.fori_loop(0, NZ * NX, step, 0)
+    def fill(n, piece):
+        for z in range(NZ):
+            for k, core in ((0, c), (1, 1 - c)):
+                row = pl.multiple_of(z * (NC * B) + core * B, B)
+                block[n, pl.ds(row, B), :] = piece(z, k)
+
+    for u in range(NM):
+        shift = shift_of(where, lax.rem(m + u, NM))
+        fill(u, lambda z, k: pack[z, 16 + NX * k + shift])
+    for n, ref in enumerate((from1, from3, from2)):
+        for j in range(2):
+            fill(4 + 2 * n + j, lambda z, k: ref[z, 2 * k + j])
+    table = (
+        ((0, 0), (1, 1), (2, 1), (3, 1)),
+        ((1, 0), (6, 0), (7, 1), (5, 0)),
+        ((2, 0), (7, 0), (8, 0), (9, 1)),
+        ((3, 0), (5, 1), (9, 0), (4, 0)),
+    )
 
     def product(basis):
-        def rows(i, carry):
-            r = pl.ds(block_start(i, W), W)
-            out[r, :] = dot_nn(stats[r, :], basis[...])
-            return carry
-
-        lax.fori_loop(0, NM, rows, 0)
+        for u in range(NM):
+            total = None
+            for v in range(NM):
+                rows = basis[pl.ds(block_start(lax.rem(m + v, NM), W), W), :]
+                place, turned = table[u][v]
+                part = (dot_tn if turned else dot_nn)(block[place], rows)
+                total = part if total is None else total + part
+            out[pl.ds(block_start(lax.rem(m + u, NM), W), W), :] = total
 
     @pl.when(c == 0)
     def _():
@@ -160,8 +201,8 @@
     def step(k, carry):
         xp, zp = k // NZ, k % NZ
         value = rot[pl.ds(pl.multiple_of(k * (NC * B) + c * B, B), B), :]
-        one = 0.9 * pack[zp, 2 * NX + xp].astype(F32) + 0.1 * value
-        two = 0.95 * pack[zp, 3 * NX + xp].astype(F32) + 0.05 * value * value
+        one = 0.9 * pack[zp, 2 * NX + shift_of(where, xp)].astype(F32) + 0.1 * value
+        two = 0.95 * pack[zp, 3 * NX + shift_of(where, xp)].astype(F32) + 0.05 * value * value
         value = (one / FIX_ONE / (jnp.sqrt(two / FIX_TWO) + 1e-08)).astype(BF)
         for copy in range(NM):
             direct[copy, pl.ds(block_start(k, B), B), :] = value
@@ -275,11 +316,12 @@
         ]
     sent[half + 2 * nb :] = got[0, half + 5 * B :]
     for t in range(NX):
-        sent[half + 2 * nb + t : half + 2 * nb + t + 1] = got[t, half + 5 * B : half + 5 * B + 1]
+        row = half + 2 * nb + 2 * t
+        sent[row : row + 2] = got[t, half + 5 * B : half + 5 * B + 2]
 
 
 def final_kernel(
-    where, got, own_slot, recv, m1, m2, sl, sr, o1, o2, osl, osr, obl, obr, slot
+    where, got, own_slot, recv, m1, m2, sl, sr, o1, o2, osl, osr, obl, obr, slot, norm
 ):
     c = where[2]
     half = own_slot.shape[0]
@@ -287,7 +329,11 @@
     slot[0, pl.ds(block_start(c, half), half)] = own_slot[...]
     slot[0, pl.ds(block_start(1 - c, half), half)] = recv[:half]
     row = pl.multiple_of(c * B, B)
+    norm_oth = recv[half + 2 * nb :].astype(F32)
     for t in range(NX):
+        norm_own = got[t, half + 5 * B :].astype(F32)
+        value = norm_own[0:2] + norm_oth[2 * t : 2 * t + 2]
+        norm[2 * t : 2 * t + 2] = jnp.where(where[8] > 0, value, 0.0)
         rot = got[t, half : half + B].astype(F32)
         o1[t] = 0.9 * m1[t] + 0.1 * rot
         o2[t] = 0.95 * m2[t] + 0.05 * rot * rot
@@ -331,30 +377,24 @@
         which = jnp.sum(jnp.where(hit, jnp.arange(NX, dtype=jnp.int32), 0))
         return [jnp.any(hit).astype(jnp.int32), which]
 
-    where = jnp.stack([xi, zi, ci, mi, *owned(mine_dp), *owned(other_dp)]).astype(jnp.int32)
+    where = jnp.stack([xi, zi, ci, mi, *owned(mine_dp), *owned(other_dp), mine_dp == owners[NX]])
+    where = where.astype(jnp.int32)
 
     with jax.named_scope("state_rows"):
-        (home,) = call(
+        home = pl.pallas_call(
             pack_kernel,
-            "pack",
-            [((NX, 6, B, W), BF)],
-            [],
-            where,
-            left_basis,
-            right_basis,
-            moment1,
-            moment2,
-            left_stats,
-            right_stats,
-        )
-        rows = exchange(home, "x")
-        stats_mine = jnp.where(left_core, rows[:, 4], rows[:, 5])
-        stats_send = jnp.where(left_core, rows[:, 5], rows[:, 4])
-        stats_recv = swap_cores(stats_send)
-        stats_rows = ordered(ci, stats_mine, stats_recv)
-        pack = jnp.concatenate(
-            [rows[:, :4].swapaxes(0, 1).reshape(16, B, W), stats_rows.reshape(8, B, W)], axis=0
-        )
+            out_shape=[jax.ShapeDtypeStruct((6, B, W), BF)] * NX,
+            in_specs=[pl.BlockSpec(memory_space=pl.ANY)] * 6,
+            out_specs=[VMEM] * NX,
+            scratch_shapes=[pltpu.VMEM((6, NX, B, W), F32), pltpu.SemaphoreType.DMA((6,))],
+            name="pack",
+        )(left_basis, right_basis, moment1, moment2, left_stats, right_stats)
+        rows = [home[0]] + [
+            lax.ppermute(home[s], "x", [(i, (i + s) % NX) for i in range(NX)]) for s in (1, 2, 3)
+        ]
+        stats_recv = swap_cores(jnp.stack([r[5] for r in rows]))
+        pack = jnp.stack([r[:5] for r in rows], axis=1).reshape(5 * NX, B, W)
+        pack = jnp.concatenate([pack, stats_recv], axis=0)
         pack = lax.all_gather(pack, "z", axis=0)
 
     with jax.named_scope("grad_sum"):
@@ -374,38 +414,34 @@
         grads_s, norm_s = partial(feat_mine, ci)
         acc = jnp.concatenate([grads_s, norm_s], axis=1) + got.astype(F32)
         acc = exchange(acc.astype(BF), "x")
-        acc, pack = lax.optimization_barrier((acc, pack))
-
-    with jax.named_scope("state_all"):
-        bases = lax.all_gather(pack[:, :8], "mp", axis=0)
-        stats = pack[:, 16:]
-        stats_all = [stats] + [
-            lax.ppermute(stats, "mp", [(i, (i + s) % NM) for i in range(NM)]) for s in (1, 2, 3)
-        ]
-        bases_other = swap_cores(bases)
-        left, right = call(
-            prep_kernel, "prep", [((full, full), BF)] * 2, [], where, bases, bases_other
-        )
-        (power_old,) = call(
-            old_power_kernel,
-            "old_power",
-            [((full, full), F32)],
-            [((full, full), BF)],
-            where,
-            *stats_all,
-            left,
-            right,
-        )
 
     with jax.named_scope("grad_sum"):
         acc = jnp.sum(acc.astype(F32), axis=0)
         norm_z = jnp.pad(acc[half].reshape(NZ, 1, 32), ((0, 0), (0, PAD - 1), (0, W - 32)))
         acc = jnp.concatenate([acc[:half].reshape(NZ, half // NZ, W), norm_z], axis=1)
         acc = exchange(acc.astype(BF), "z")
+        acc, pack = lax.optimization_barrier((acc, pack))
         acc = jnp.sum(acc.astype(F32), axis=0)
         grad_rows = acc[: half // NZ].astype(BF)
         norm_total = acc[half // NZ, :32]
 
+    with jax.named_scope("state_all"):
+        piece = (NZ, 4, B, W)
+        bases, near, far = call(
+            select_kernel,
+            "select",
+            [((NZ, 8, B, W), BF), (piece, BF), (piece, BF)],
+            [],
+            where,
+            pack,
+        )
+        bases = lax.all_gather(bases, "mp", axis=0)
+
+        def turn(value, s):
+            return lax.ppermute(value, "mp", [(i, (i + s) % NM) for i in range(NM)])
+
+        stats = [turn(far, 1), turn(near, 3), turn(near, 2)]
+
     new_nm = 0.9 * norm_m + 0.1 * norm_total
     new_nv = 0.95 * norm_v + 0.05 * norm_total * norm_total
     norm_step = new_nm / FIX_ONE / (jnp.sqrt(new_nv / FIX_TWO) + 1e-08)
@@ -413,10 +449,17 @@
     with jax.named_scope("grad_all"):
         norm_row = jnp.pad(norm_step.astype(BF)[None], ((0, PAD - 1), (0, W - 32)))
         grad_z = everyone(jnp.concatenate([grad_rows, norm_row], axis=0), "z", NZ)
-        norm_zs = grad_z[:, half // NZ, :32].reshape(1, W)
+        norm_zs = grad_z[:, half // NZ, None, :32]
+        norm_zs = jnp.where(jnp.arange(NC)[None, :, None] == ci, norm_zs, 0).reshape(2, W)
         grad_half = grad_z[:, : half // NZ].reshape(half, W)
+        grad_half, *stats = lax.optimization_barrier((grad_half, *stats))
         grad_half = everyone(grad_half, "mp", NM)
+        grad_half, bases = lax.optimization_barrier((grad_half, bases))
         grad_other = swap_cores(grad_half)
+        bases_other = swap_cores(bases)
+        left, right = call(
+            prep_kernel, "prep", [((full, full), BF)] * 2, [], where, bases, bases_other
+        )
 
     with jax.named_scope("rotate"):
         grad, work, direction, rot_home = call(
@@ -438,6 +481,18 @@
         )
         direction = exchange(direction, "mp")
     with jax.named_scope("power"):
+        (power_old,) = call(
+            old_power_kernel,
+            "old_power",
+            [((full, full), F32)],
+            [((10, W, W), BF)],
+            where,
+            pack,
+            *stats,
+            left,
+            right,
+            cost=COST,
+        )
         outer, basis = call(
             power_kernel,
             "power",
@@ -447,11 +502,13 @@
             grad,
             work,
             power_old,
-        )
+            cost=COST,
+        )
+        direction, outer, basis = lax.optimization_barrier((direction, outer, basis))
     with jax.named_scope("update"):
         (back,) = call(back_kernel, "back", [((half, W), BF)], [], where, direction, right)
         back_other = swap_cores(back)
-        norm_pad = jnp.pad(norm_zs, ((0, PAD - 1), (0, 0)))
+        norm_pad = jnp.pad(norm_zs, ((0, PAD - 2), (0, 0)))
         (sent,) = call(
             update_kernel,
             "update",
@@ -483,7 +540,7 @@
         outs = call(
             final_kernel,
             "final",
-            [state] * 6 + [((1, full, W), BF)],
+            [state] * 6 + [((1, full, W), BF), ((2 * NX, W), F32)],
             [],
             where,
             got,
@@ -494,11 +551,8 @@
             left_stats,
             right_stats,
         )
-        norm_xz = got[:, half + 5 * B]
-        norm_all = ordered(ci, norm_xz, recv[half + 2 * nb : half + 2 * nb + NX])
-        norm_all = norm_all.reshape(NC, NX, NZ, 32).transpose(1, 2, 0, 3).reshape(1, -1)
-        norm_slot = jnp.where(mine_dp == owners[NX], norm_all.astype(F32), 0.0)
-    return (*outs, new_nm, new_nv, norm_slot)
+    *outs, norm_slot = outs
+    return (*outs, new_nm, new_nv, norm_slot.reshape(1, -1))
 
 
 def solution(mesh):

time: 249 us -> 212 us (0.85)
  waiting for transfers between devices: 63.5 us -> 30.8 us
  starting transfers between devices: 23 us -> 33.4 us
  blocking collectives: 68.7 us -> 58.5 us
    all_gather x1, waiting for transfers between devices: 17.3 us -> 0.01 us  [shards(): bases = lax.all_gather(bases, 'mp', axis=0)]
    all_gather x1, waiting for transfers between devices: 11.9 us -> 0.01 us  [shards(): pack = lax.all_gather(pack, 'z', axis=0)]
    ppermute x3 -> x6, waiting for transfers between devices: 18.1 us -> 6.89 us  [the longest x3 6.88 us: turn(): return lax.ppermute(value, 'mp', [(i, (i + s) % NM) for i in range(NM)])]
    all_to_all x4 -> x3, blocking collectives: 68.7 us -> 58.5 us  [exchange(): return lax.all_to_all(value, axis, 0, 0, tiled=True)]
    ppermute x6, waiting for transfers between devices: 1.08 us -> 9.38 us  [swap_cores(): return lax.ppermute(value, 'c', [(0, 1), (1, 0)])]
    ppermute x3 -> x6, starting transfers between devices: 3.79 us -> 11.2 us  [the longest x3 5.72 us: shards(): lax.ppermute(home[s], 'x', [(i, (i + s) % NX) for i in range(NX)])]
    all_to_all x3, starting transfers between devices: 11.8 us -> 15.4 us  [exchange(): return lax.all_to_all(value, axis, 0, 0, tiled=True)]
    unnamed x55 -> x61, local copies, waits for them, and re-layouts: 16 us -> 19.3 us
  transfers between devices with their start and end apart: 14 -> 17, of which waited for: 9 -> 8; matrix products, arithmetic and copies ran while one was open for 5% -> 8% of each run, Pallas kernels for 8% -> 8%
where the time goes in v1:
time: 212 us; the launch traced here: 210 us
  blocking collectives  58.5 us (28%)
  Pallas kernels  35.6 us (17%)
  starting transfers between devices  33.4 us (16%)
  waiting for transfers between devices  30.8 us (15%)
  local copies, waits for them, and re-layouts  24.3 us (11%)
  between operations  16.5 us (8%)
  other arithmetic  6.42 us (3%)
  matrix products  4.99 us (2%)
    all_to_all x3, blocking collectives, exchange(): return lax.all_to_all(value, axis, 0, 0, tiled=True)  58.5 us
    pallas_call x9, Pallas kernels, call(): pl.pallas_call(kernel, out_shape=[jax.ShapeDtypeStruct(s, d) for s, d in...  33.7 us
    unnamed x61, local copies, waits for them, and re-layouts  19.3 us
    all_to_all x3, starting transfers between devices, exchange(): return lax.all_to_all(value, axis, 0, 0, tiled=True)  15.4 us
    all_to_all x3, waiting for transfers between devices, exchange(): return lax.all_to_all(value, axis, 0, 0, tiled=True)  14.5 us
    ppermute x6, waiting for transfers between devices, swap_cores(): return lax.ppermute(value, 'c', [(0, 1), (1, 0)])  9.38 us
    ppermute x3, waiting for transfers between devices, turn(): return lax.ppermute(value, 'mp', [(i, (i + s) % NM) for i in range(NM)])  6.88 us
    ppermute x6, starting transfers between devices, swap_cores(): return lax.ppermute(value, 'c', [(0, 1), (1, 0)])  6.69 us
  transfers between devices with their start and end apart: 17, of which 8 were waited for; matrix products, arithmetic and copies ran while one was open for 8% of the time, Pallas kernels for 8%

profile of v1, /device:TPU:1, one launch (start us, length us, event | category | flops | bytes accessed | tf_op | source)
XLA Modules:
  0.0 210.5 jit_solution(14746097177014816896)
XLA Ops:
  7.2 1.9 pack.1
  9.1 2.1 %collective-permute-start.1 = (bf16[6,16,256]{2,1,0:T(8,128)(2,1)}, bf16[6,16,256]{2,1,0:T(8,128)(2,1)S(1)}, u32[]{:S(2)}, u32[]{:S(2)}) collective-permute-start(bf16[6,16,256]{2,1,0:T(8,128)(2,1)} %get-tuple-element.47), channel_id=1, source_target_pairs={{0,64},{64,128},{128,192},{192,0},{1,65},{65,129},{129,193},{193,1... | collective-permute-start | bytes 147464 | tf_op jit(solution)/shard_map/state_rows/ppermute | solution.py:393
  11.2 2.5 %collective-permute-start.2 = (bf16[6,16,256]{2,1,0:T(8,128)(2,1)}, bf16[6,16,256]{2,1,0:T(8,128)(2,1)S(1)}, u32[]{:S(2)}, u32[]{:S(2)}) collective-permute-start(bf16[6,16,256]{2,1,0:T(8,128)(2,1)} %get-tuple-element.48), channel_id=1, source_target_pairs={{0,128},{64,192},{128,0},{192,64},{1,129},{65,193},{129,1},{193,65... | collective-permute-start | bytes 147464 | tf_op jit(solution)/shard_map/state_rows/ppermute | solution.py:393
  13.7 1.2 collective-permute-start.3
  15.4 1.4 reduce.6
  17.0 2.5 %fusion.13 = bf16[4,512,256]{2,1,0:T(8,128)(2,1)S(1)} fusion(bf16[1024,4,256]{2,1,0:T(4,128)(2,1)S(1)} %copy-done, bf16[1024,1024]{1,0:T(8,128)(2,1)} %param.12, s32[]{:T(128)S(6)} %select_n.32), kind=kOutput, calls=%fused_computation.11 | convolution fusion | flops 1074266112 | bytes 4194308 | tf_op jit(solution)/shard_map/grad_sum/ti,tnc->nic/dot_general | solution.py:406
  19.5 1.1 fusion.16
  20.6 1.5 collective-permute-start
  22.4 2.1 collective-permute-done.4
  24.5 0.7 pad_maximum_fusion
  25.2 2.5 %fusion.7 = f32[4,512,256]{2,1,0:T(8,128)S(1)} fusion(bf16[1024,4,256]{2,1,0:T(4,128)(2,1)S(1)} %copy-done, bf16[1024,1024]{1,0:T(8,128)(2,1)} %param.12, s32[]{:T(128)S(6)} %select_n.30), kind=kOutput, calls=%fused_computation.9 | convolution fusion | flops 1073741824 | bytes 5242884 | tf_op jit(solution)/shard_map/grad_sum/ti,tnc->nic/dot_general | solution.py:406
  28.0 17.9 %all_to_all.30 = bf16[4,528,256]{2,1,0:T(8,128)(2,1)S(1)} all-to-all(bf16[4,528,256]{2,1,0:T(8,128)(2,1)S(1)} %fusion.1), channel_id=1, replica_groups=mesh['x'=4,'z'=8,'c'=2,'mp'=4] {'x'}, dimensions={0} | all-to-all | bytes 2162688 | tf_op jit(solution)/shard_map/grad_sum/all_to_all | solution.py:29
  46.4 0.8 fusion.22
  47.1 7.7 %all-to-all-start.1 = ((bf16[8,80,256]{2,1,0:T(8,128)(2,1)}), bf16[8,80,256]{2,1,0:T(8,128)(2,1)S(1)}, u32[]{:S(2)}, u32[]{:S(2)}) async-start(bf16[8,80,256]{2,1,0:T(8,128)(2,1)} %fusion.22), calls=%async_computation.1 | async-start | bytes 655360 | tf_op jit(solution)/shard_map/grad_sum/all_to_all | solution.py:29
  54.9 0.6 slice.52
  56.2 0.6 compare_reduce_fusion
  58.1 0.6 fusion.29
  58.7 1.4 stack.69.where
  60.1 8.9 %all-to-all-done.1 = bf16[8,80,256]{2,1,0:T(8,128)(2,1)S(1)} async-done(((bf16[8,80,256]{2,1,0:T(8,128)(2,1)}), bf16[8,80,256]{2,1,0:T(8,128)(2,1)S(1)}, u32[]{:S(2)}, u32[]{:S(2)}) %all-to-all-start.1) | async-done | bytes 327712 | tf_op jit(solution)/shard_map/grad_sum/all_to_all | solution.py:29
  69.0 1.4 copy-done.6
  70.4 1.4 select.24
  71.9 0.5 convert_bitcast_fusion
  72.4 0.8 broadcast_in_dim.45
  73.2 4.1 %all-to-all-start.2 = ((bf16[8,80,256]{2,1,0:T(8,128)(2,1)}), bf16[8,80,256]{2,1,0:T(8,128)(2,1)}, u32[]{:S(2)}, u32[]{:S(2)}) async-start(bf16[8,80,256]{2,1,0:T(8,128)(2,1)} %broadcast_in_dim.45), calls=%async_computation.2 | async-start | bytes 655360 | tf_op jit(solution)/shard_map/grad_all/all_to_all | solution.py:29
  77.3 1.8 collective-permute-start.5
  79.1 2.4 %collective-permute-start.7 = (bf16[8,4,16,256]{3,2,1,0:T(8,128)(2,1)S(1)}, bf16[8,4,16,256]{3,2,1,0:T(8,128)(2,1)S(1)}, u32[]{:S(2)}, u32[]{:S(2)}) collective-permute-start(bf16[8,4,16,256]{3,2,1,0:T(8,128)(2,1)S(1)} %get-tuple-element.53), channel_id=1, source_target_pairs={{0,2},{1,3},{2,0},{3,1},{4,6},{5,7},{6,4},{7,5},{8,10},{9,11},{10,... | collective-permute-start | bytes 786440 | tf_op jit(solution)/shard_map/state_all/ppermute | solution.py:441
  81.5 1.3 collective-permute-start.6
  82.8 5.6 %all-to-all-done.2 = bf16[8,80,256]{2,1,0:T(8,128)(2,1)} async-done(((bf16[8,80,256]{2,1,0:T(8,128)(2,1)}), bf16[8,80,256]{2,1,0:T(8,128)(2,1)}, u32[]{:S(2)}, u32[]{:S(2)}) %all-to-all-start.2) | async-done | bytes 327712 | tf_op jit(solution)/shard_map/grad_all/all_to_all | solution.py:29
  88.4 1.0 slice.77
  89.4 0.7 copy-done.18
  90.1 5.9 %collective-permute-done.7.from2 = bf16[8,4,16,256]{3,2,1,0:T(8,128)(2,1)S(1)} collective-permute-done((bf16[8,4,16,256]{3,2,1,0:T(8,128)(2,1)S(1)}, bf16[8,4,16,256]{3,2,1,0:T(8,128)(2,1)S(1)}, u32[]{:S(2)}, u32[]{:S(2)}) %collective-permute-start.7) | collective-permute-done | bytes 262176 | tf_op jit(solution)/shard_map/state_all/ppermute | solution.py:441
  96.0 0.7 copy-done.20
  96.7 1.0 collective-permute-done.6.from3
  97.7 0.7 copy-done.22
  98.5 20.7 %all_to_all.31.own = bf16[4,512,256]{2,1,0:T(8,128)(2,1)S(1)} all-to-all(bf16[4,512,256]{2,1,0:T(8,128)(2,1)S(1)} %broadcast_in_dim.46), channel_id=1, replica_groups=mesh['x'=4,'z'=8,'c'=2,'mp'=4] {'mp'}, dimensions={0} | all-to-all | bytes 2097152 | tf_op jit(solution)/shard_map/grad_all/all_to_all | solution.py:29
  119.2 3.2 %collective-permute-start.9 = (bf16[4,8,8,16,256]{4,3,2,1,0:T(8,128)(2,1)}, bf16[4,8,8,16,256]{4,3,2,1,0:T(8,128)(2,1)S(1)}, u32[]{:S(2)}, u32[]{:S(2)}) collective-permute-start(bf16[4,8,8,16,256]{4,3,2,1,0:T(8,128)(2,1)} %bitcast.65), channel_id=1, source_target_pairs={{0,4},{4,0},{1,5},{5,1},{2,6},{6,2},{3,7},{7,3},{8,12},{12,8},{9,1... | collective-permute-start | bytes 6291464 | tf_op jit(solution)/shard_map/grad_all/ppermute | solution.py:25
  122.6 5.4 %collective-permute-done.9.oth = bf16[4,8,8,16,256]{4,3,2,1,0:T(8,128)(2,1)S(1)} collective-permute-done((bf16[4,8,8,16,256]{4,3,2,1,0:T(8,128)(2,1)}, bf16[4,8,8,16,256]{4,3,2,1,0:T(8,128)(2,1)S(1)}, u32[]{:S(2)}, u32[]{:S(2)}) %collective-permute-start.9) | collective-permute-done | bytes 2097184 | tf_op jit(solution)/shard_map/grad_all/ppermute | solution.py:25
  128.0 1.3 copy-done.24
  129.3 2.9 %prep.1 = (bf16[1024,1024]{1,0:T(8,128)(2,1)S(1)}, bf16[1024,1024]{1,0:T(8,128)(2,1)S(1)}) custom-call(s32[9]{0:T(128)S(1)} %stack.69.where, bf16[4,8,8,16,256]{4,3,2,1,0:T(8,128)(2,1)} %bitcast.66, bf16[4,8,8,16,256]{4,3,2,1,0:T(8,128)(2,1)} %copy-done.24), custom_call_target="tpu_custom_call" | custom-call | tf_op jit(solution)/shard_map/grad_all/prep/pallas_call | solution.py:61
  132.2 1.4 copy-done.1
  133.6 1.4 copy-done.4
  135.0 10.2 %rotate.1 = (bf16[1024,1024]{1,0:T(8,128)(2,1)}, bf16[1024,1024]{1,0:T(8,128)(2,1)}, bf16[4,512,256]{2,1,0:T(8,128)(2,1)S(1)}, bf16[4,16,256]{2,1,0:T(8,128)(2,1)S(1)}) custom-call(s32[9]{0:T(128)S(1)} %stack.69.where, bf16[4,512,256]{2,1,0:T(8,128)(2,1)S(1)} %all_to_all.31.own, bf16[4,512,256]{2,1,0:T(8,128)(2,1)S(1)} %collective-permute-done.8.oth, ...), custom_call_target="tpu_custom_call" | custom-call | tf_op jit(solution)/shard_map/rotate/rotate/pallas_call | solution.py:61
  145.2 1.0 copy-done.9
  146.2 0.6 copy-done.14
  146.8 3.6 %all-to-all-start.4 = ((bf16[4,512,256]{2,1,0:T(8,128)(2,1)}), bf16[4,512,256]{2,1,0:T(8,128)(2,1)S(1)}, u32[]{:S(2)}, u32[]{:S(2)}) async-start(bf16[4,512,256]{2,1,0:T(8,128)(2,1)} %copy-done.9), calls=%async_computation.4 | async-start | bytes 2097152 | tf_op jit(solution)/shard_map/rotate/all_to_all | solution.py:29
  150.5 1.6 copy-done.2
  152.1 1.4 copy-done.8
  153.5 0.9 copy-done.21
  154.5 0.9 copy-done.23
  155.4 6.2 %old_power.1.old = f32[1024,1024]{1,0:T(8,128)} custom-call(s32[9]{0:T(128)S(1)} %stack.69.where, bf16[8,24,16,256]{3,2,1,0:T(8,128)(2,1)S(1)} %bitcast.63, bf16[8,4,16,256]{3,2,1,0:T(8,128)(2,1)S(1)} %copy-done.19, bf16[8,4,16,256]{3,2,1,0:T(8,128)(2,1)S(1)} %copy-done.23, bf16[8,4,16,256]{3,2,1,0:T(8,128)(2,1)S(1)} %copy-done.21, ...), custom_call_target="tpu_custom_call" | custom-call | flops 6000000000 | bytes 24000000 | tf_op jit(solution)/shard_map/power/old_power/pallas_call | solution.py:61
  161.6 8.6 %power.1 = (bf16[4,32,256]{2,1,0:T(8,128)(2,1)S(1)}, bf16[4,32,256]{2,1,0:T(8,128)(2,1)S(1)}) custom-call(s32[9]{0:T(128)S(1)} %stack.69.where, bf16[1024,1024]{1,0:T(8,128)(2,1)S(1)} %copy-done.16, bf16[1024,1024]{1,0:T(8,128)(2,1)S(1)} %copy-done.17, f32[1024,1024]{1,0:T(8,128)} %old_power.1.old), custom_call_target="tpu_custom_call" | custom-call | flops 6000000000 | bytes 24000000 | tf_op jit(solution)/shard_map/power/power/pallas_call | solution.py:61
  170.2 1.6 copy-done.5
  171.8 1.0 back.1.own
  172.9 0.7 slice.78
  173.8 0.6 collective-permute-done.10.oth
  174.4 1.6 copy-done.3
  176.0 0.8 copy-done.15
  176.8 1.2 update.1
  178.1 19.8 %all_to_all.32.got = bf16[4,608,256]{2,1,0:T(8,128)(2,1)S(1)} all-to-all(bf16[4,608,256]{2,1,0:T(8,128)(2,1)S(1)} %update.1), channel_id=1, replica_groups=mesh['x'=4,'z'=8,'c'=2,'mp'=4] {'x'}, dimensions={0} | all-to-all | bytes 2490368 | tf_op jit(solution)/shard_map/home/all_to_all | solution.py:29
  197.9 0.6 relay.1
  198.6 1.7 collective-permute-start.11
  200.2 1.3 collective-permute-done.11.recv
  201.5 1.5 final.1
  203.0 0.6 copy.84
  (89 shorter events, 2.4 us)
Async XLA Ops:
  7.2 9.8 %copy-start = (bf16[1024,4,256]{2,1,0:T(4,128)(2,1)S(1)}, bf16[1024,4,256]{2,1,0:T(4,128)(2,1)}, u32[]{:S(2)}) copy-start(bf16[1024,4,256]{2,1,0:T(4,128)(2,1)} %param.13) | copy-start | bytes 6291460
  7.2 61.8 %all-gather.5.cloned.1.call-start = ((), (), s32[]{:S(2)}) async-start(), calls=%async_computation.6 | async-start | bytes 1769472 | tf_op jit(solution)/shard_map/state_rows/all_gather | solution.py:398
  9.1 13.0 %collective-permute-start.1 = (bf16[6,16,256]{2,1,0:T(8,128)(2,1)}, bf16[6,16,256]{2,1,0:T(8,128)(2,1)S(1)}, u32[]{:S(2)}, u32[]{:S(2)}) collective-permute-start(bf16[6,16,256]{2,1,0:T(8,128)(2,1)} %get-tuple-element.47), channel_id=1, source_target_pairs={{0,64},{64,128},{128,192},{192,0},{1,65},{65,129},{129,193},{193,1... | collective-permute-start | bytes 147464 | tf_op jit(solution)/shard_map/state_rows/ppermute | solution.py:393
  11.2 10.9 %collective-permute-start.2 = (bf16[6,16,256]{2,1,0:T(8,128)(2,1)}, bf16[6,16,256]{2,1,0:T(8,128)(2,1)S(1)}, u32[]{:S(2)}, u32[]{:S(2)}) collective-permute-start(bf16[6,16,256]{2,1,0:T(8,128)(2,1)} %get-tuple-element.48), channel_id=1, source_target_pairs={{0,128},{64,192},{128,0},{192,64},{1,129},{65,193},{129,1},{193,65... | collective-permute-start | bytes 147464 | tf_op jit(solution)/shard_map/state_rows/ppermute | solution.py:393
  13.7 8.4 %collective-permute-start.3 = (bf16[6,16,256]{2,1,0:T(8,128)(2,1)}, bf16[6,16,256]{2,1,0:T(8,128)(2,1)S(1)}, u32[]{:S(2)}, u32[]{:S(2)}) collective-permute-start(bf16[6,16,256]{2,1,0:T(8,128)(2,1)} %get-tuple-element.49), channel_id=1, source_target_pairs={{0,192},{64,0},{128,64},{192,128},{1,193},{65,1},{129,65},{193,129... | collective-permute-start | bytes 147464 | tf_op jit(solution)/shard_map/state_rows/ppermute | solution.py:393
  19.5 2.6 %copy-start.25 = (bf16[6,16,256]{2,1,0:T(8,128)(2,1)S(1)}, bf16[6,16,256]{2,1,0:T(8,128)(2,1)}, u32[]{:S(2)}) copy-start(bf16[6,16,256]{2,1,0:T(8,128)(2,1)} %get-tuple-element.46) | copy-start | bytes 147460
  20.6 7.2 %collective-permute-start = (bf16[4,528,256]{2,1,0:T(8,128)(2,1)}, bf16[4,528,256]{2,1,0:T(8,128)(2,1)S(1)}, u32[]{:S(2)}, u32[]{:S(2)}) collective-permute-start(bf16[4,528,256]{2,1,0:T(8,128)(2,1)} %fusion.16), channel_id=1, source_target_pairs={{0,4},{4,0},{1,5},{5,1},{2,6},{6,2},{3,7},{7,3},{8,12},{12,8},{9,1... | collective-permute-start | bytes 3244040 | tf_op jit(solution)/shard_map/grad_sum/ppermute | solution.py:25
  22.2 2.3 %collective-permute-start.4 = (bf16[4,16,256]{2,1,0:T(8,128)(2,1)S(1)}, bf16[4,16,256]{2,1,0:T(8,128)(2,1)S(1)}, u32[]{:S(2)}, u32[]{:S(2)}) collective-permute-start(bf16[4,16,256]{2,1,0:T(8,128)(2,1)S(1)} %pad_maximum_fusion.2), channel_id=1, source_target_pairs={{0,4},{4,0},{1,5},{5,1},{2,6},{6,2},{3,7},{7,3},{8,12},{12,8},{9,1... | collective-permute-start | bytes 98312 | tf_op jit(solution)/shard_map/state_rows/ppermute | solution.py:25
  46.0 9.0 %copy-start.26 = (s32[5]{0:T(128)S(1)}, s32[5]{0:T(128)}, u32[]{:S(2)}) copy-start(s32[5]{0:T(128)} %param.15) | copy-start | bytes 64
  46.2 25.7 %copy-start.27 = (f32[32]{0:T(128)S(1)}, f32[32]{0:T(128)}, u32[]{:S(2)}) copy-start(f32[32]{0:T(128)} %param.22) | copy-start | bytes 388
  46.2 25.7 %copy-start.28 = (f32[32]{0:T(128)S(1)}, f32[32]{0:T(128)}, u32[]{:S(2)}) copy-start(f32[32]{0:T(128)} %param.23) | copy-start | bytes 388
  47.1 21.8 %all-to-all-start.1 = ((bf16[8,80,256]{2,1,0:T(8,128)(2,1)}), bf16[8,80,256]{2,1,0:T(8,128)(2,1)S(1)}, u32[]{:S(2)}, u32[]{:S(2)}) async-start(bf16[8,80,256]{2,1,0:T(8,128)(2,1)} %fusion.22), calls=%async_computation.1 | async-start | bytes 655360 | tf_op jit(solution)/shard_map/grad_sum/all_to_all | solution.py:29
  54.9 64.4 %all-gather.7.cloned.1.call-start = ((), (), s32[]{:S(2)}) async-start(), calls=%async_computation.7 | async-start | bytes 2621440 | tf_op jit(solution)/shard_map/state_all/all_gather | solution.py:438
  69.0 1.4 copy-start.6
  73.2 15.2 %all-to-all-start.2 = ((bf16[8,80,256]{2,1,0:T(8,128)(2,1)}), bf16[8,80,256]{2,1,0:T(8,128)(2,1)}, u32[]{:S(2)}, u32[]{:S(2)}) async-start(bf16[8,80,256]{2,1,0:T(8,128)(2,1)} %broadcast_in_dim.45), calls=%async_computation.2 | async-start | bytes 655360 | tf_op jit(solution)/shard_map/grad_all/all_to_all | solution.py:29
  77.3 12.1 %collective-permute-start.5 = (bf16[8,4,16,256]{3,2,1,0:T(8,128)(2,1)S(1)}, bf16[8,4,16,256]{3,2,1,0:T(8,128)(2,1)S(1)}, u32[]{:S(2)}, u32[]{:S(2)}) collective-permute-start(bf16[8,4,16,256]{3,2,1,0:T(8,128)(2,1)S(1)} %get-tuple-element.52), channel_id=1, source_target_pairs={{0,1},{1,2},{2,3},{3,0},{4,5},{5,6},{6,7},{7,4},{8,9},{9,10},{10,1... | collective-permute-start | bytes 786440 | tf_op jit(solution)/shard_map/state_all/ppermute | solution.py:441
  79.1 16.9 %collective-permute-start.7 = (bf16[8,4,16,256]{3,2,1,0:T(8,128)(2,1)S(1)}, bf16[8,4,16,256]{3,2,1,0:T(8,128)(2,1)S(1)}, u32[]{:S(2)}, u32[]{:S(2)}) collective-permute-start(bf16[8,4,16,256]{3,2,1,0:T(8,128)(2,1)S(1)} %get-tuple-element.53), channel_id=1, source_target_pairs={{0,2},{1,3},{2,0},{3,1},{4,6},{5,7},{6,4},{7,5},{8,10},{9,11},{10,... | collective-permute-start | bytes 786440 | tf_op jit(solution)/shard_map/state_all/ppermute | solution.py:441
  81.5 16.2 %collective-permute-start.6 = (bf16[8,4,16,256]{3,2,1,0:T(8,128)(2,1)S(1)}, bf16[8,4,16,256]{3,2,1,0:T(8,128)(2,1)S(1)}, u32[]{:S(2)}, u32[]{:S(2)}) collective-permute-start(bf16[8,4,16,256]{3,2,1,0:T(8,128)(2,1)S(1)} %get-tuple-element.53), channel_id=1, source_target_pairs={{0,3},{1,0},{2,1},{3,2},{4,7},{5,4},{6,5},{7,6},{8,11},{9,8},{10,9... | collective-permute-start | bytes 786440 | tf_op jit(solution)/shard_map/state_all/ppermute | solution.py:441
  89.4 0.7 copy-start.18
  96.0 0.7 copy-start.20
  97.7 0.7 copy-start.22
  119.2 15.8 %copy-start.7 = (bf16[192,16,256]{2,1,0:T(8,128)(2,1)S(1)}, bf16[192,16,256]{2,1,0:T(8,128)(2,1)}, u32[]{:S(2)}) copy-start(bf16[192,16,256]{2,1,0:T(8,128)(2,1)} %all-gather.5.cloned.1.call-done) | copy-start | bytes 4718596
  119.2 8.7 %collective-permute-start.9 = (bf16[4,8,8,16,256]{4,3,2,1,0:T(8,128)(2,1)}, bf16[4,8,8,16,256]{4,3,2,1,0:T(8,128)(2,1)S(1)}, u32[]{:S(2)}, u32[]{:S(2)}) collective-permute-start(bf16[4,8,8,16,256]{4,3,2,1,0:T(8,128)(2,1)} %bitcast.65), channel_id=1, source_target_pairs={{0,4},{4,0},{1,5},{5,1},{2,6},{6,2},{3,7},{7,3},{8,12},{12,8},{9,1... | collective-permute-start | bytes 6291464 | tf_op jit(solution)/shard_map/grad_all/ppermute | solution.py:25
  122.5 12.5 %collective-permute-start.8 = (bf16[4,512,256]{2,1,0:T(8,128)(2,1)S(1)}, bf16[4,512,256]{2,1,0:T(8,128)(2,1)S(1)}, u32[]{:S(2)}, u32[]{:S(2)}) collective-permute-start(bf16[4,512,256]{2,1,0:T(8,128)(2,1)S(1)} %all_to_all.31.own), channel_id=1, source_target_pairs={{0,4},{4,0},{1,5},{5,1},{2,6},{6,2},{3,7},{7,3},{8,12},{12,8},{9,1... | collective-permute-start | bytes 3145736 | tf_op jit(solution)/shard_map/grad_all/ppermute | solution.py:25
  128.0 1.3 copy-start.24
  132.2 1.4 copy-start.1
  133.6 1.4 copy-start.4
  145.2 1.0 copy-start.9
  146.2 0.6 copy-start.14
  146.8 3.7 %copy-start.19 = (bf16[8,4,16,256]{3,2,1,0:T(8,128)(2,1)S(1)}, bf16[8,4,16,256]{3,2,1,0:T(8,128)(2,1)}, u32[]{:S(2)}) copy-start(bf16[8,4,16,256]{3,2,1,0:T(8,128)(2,1)} %copy-done.18) | copy-start | bytes 786436
  146.8 23.3 %all-to-all-start.4 = ((bf16[4,512,256]{2,1,0:T(8,128)(2,1)}), bf16[4,512,256]{2,1,0:T(8,128)(2,1)S(1)}, u32[]{:S(2)}, u32[]{:S(2)}) async-start(bf16[4,512,256]{2,1,0:T(8,128)(2,1)} %copy-done.9), calls=%async_computation.4 | async-start | bytes 2097152 | tf_op jit(solution)/shard_map/rotate/all_to_all | solution.py:29
  150.5 1.6 copy-start.2
  152.1 1.4 copy-start.8
  153.5 0.9 copy-start.21
  154.4 0.9 copy-start.23
  155.4 6.2 %copy-start.16 = (bf16[1024,1024]{1,0:T(8,128)(2,1)S(1)}, bf16[1024,1024]{1,0:T(8,128)(2,1)}, u32[]{:S(2)}) copy-start(bf16[1024,1024]{1,0:T(8,128)(2,1)} %get-tuple-element.61.grad) | copy-start | bytes 6291460
  155.4 6.2 %copy-start.17 = (bf16[1024,1024]{1,0:T(8,128)(2,1)S(1)}, bf16[1024,1024]{1,0:T(8,128)(2,1)}, u32[]{:S(2)}) copy-start(bf16[1024,1024]{1,0:T(8,128)(2,1)} %get-tuple-element.62.work) | copy-start | bytes 6291460
  170.2 1.6 copy-start.5
  172.8 1.6 collective-permute-start.10
  174.4 1.6 copy-start.3
  176.0 0.8 copy-start.15
  178.0 23.4 %copy-start.10 = (f32[4,16,256]{2,1,0:T(8,128)S(1)}, f32[4,16,256]{2,1,0:T(8,128)}, u32[]{:S(2)}) copy-start(f32[4,16,256]{2,1,0:T(8,128)} %m1.1) | copy-start | bytes 196612
  178.0 23.4 %copy-start.11 = (f32[4,16,256]{2,1,0:T(8,128)S(1)}, f32[4,16,256]{2,1,0:T(8,128)}, u32[]{:S(2)}) copy-start(f32[4,16,256]{2,1,0:T(8,128)} %m2.1) | copy-start | bytes 196612
  178.1 23.4 %copy-start.12 = (f32[4,16,256]{2,1,0:T(8,128)S(1)}, f32[4,16,256]{2,1,0:T(8,128)}, u32[]{:S(2)}) copy-start(f32[4,16,256]{2,1,0:T(8,128)} %sl.1) | copy-start | bytes 196612
  178.1 23.4 %copy-start.13 = (f32[4,16,256]{2,1,0:T(8,128)S(1)}, f32[4,16,256]{2,1,0:T(8,128)}, u32[]{:S(2)}) copy-start(f32[4,16,256]{2,1,0:T(8,128)} %sr.1) | copy-start | bytes 196612
  198.6 2.9 %collective-permute-start.11 = (bf16[656,256]{1,0:T(8,128)(2,1)S(1)}, bf16[656,256]{1,0:T(8,128)(2,1)S(1)}, u32[]{:S(2)}, u32[]{:S(2)}) collective-permute-start(bf16[656,256]{1,0:T(8,128)(2,1)S(1)} %get-tuple-element.73), channel_id=1, source_target_pairs={{0,4},{4,0},{1,5},{5,1},{2,6},{6,2},{3,7},{7,3},{8,12},{12,8},{9,1... | collective-permute-start | bytes 1007624 | tf_op jit(solution)/shard_map/home/ppermute | solution.py:25
Sparse Core Ops, SparseCore 0:
  25.3 39.2 all-gather.4
  71.9 43.3 all-gather.6

commit v2 on v1

--- a/solution.py
+++ b/solution.py
@@ -27,6 +27,10 @@
 
 def exchange(value, axis):
     return lax.all_to_all(value, axis, 0, 0, tiled=True)
+
+
+def turn(value, s):
+    return lax.ppermute(value, "mp", [(i, (i + s) % NM) for i in range(NM)])
 
 
 def everyone(value, axis, count):
@@ -87,42 +91,67 @@
         out[5] = jnp.where(c == 0, rights, lefts).astype(BF)
 
 
+def join_kernel(*refs):
+    *parts, out = refs
+    start = 0
+    for part in parts:
+        out[start : start + part.shape[0]] = part[...]
+        start += part.shape[0]
+
+
+def join(*parts):
+    shape = (sum(p.shape[0] for p in parts), *parts[0].shape[1:])
+    return pl.pallas_call(
+        join_kernel,
+        out_shape=jax.ShapeDtypeStruct(shape, parts[0].dtype),
+        in_specs=[VMEM] * len(parts),
+        out_specs=VMEM,
+        name="join",
+    )(*parts)
+
+
+def spread_kernel(r0, r1, r2, r3, other, bases, moments, stats, near, far):
+    rows = (r0, r1, r2, r3)
+    x, m = lax.axis_index("x"), lax.axis_index("mp")
+    for s, ref in enumerate(rows):
+        for k in range(2):
+            bases[NX * k + s] = ref[k]
+            moments[NX * k + s] = ref[2 + k]
+        stats[s] = ref[4]
+        stats[NX + s] = other[s]
+    for out, steps in ((near, (0, 1)), (far, (0, 2))):
+        for j, step in enumerate(steps):
+            shift = lax.rem(x - lax.rem(m + step, NM) + NX, NX)
+            for core in range(NC):
+                out[2 * core + j] = stats[NX * core + shift]
+
+
+def block_start(index, size):
+    return pl.multiple_of(index * size, size)
+
+
 def shift_of(where, xp):
     return lax.rem(where[0] - xp + NX, NX)
 
 
-def select_kernel(where, pack, bases, near, far):
-    m = where[3]
-    bases[...] = pack[:, 0:8]
-    for out, steps in ((near, (0, 1)), (far, (0, 2))):
-        for j, step in enumerate(steps):
-            shift = shift_of(where, lax.rem(m + step, NM))
-            for core in range(NC):
-                out[:, 2 * core + j] = pack[:, 16 + NX * core + shift]
-
-
-def block_start(index, size):
-    return pl.multiple_of(index * size, size)
-
-
 def prep_kernel(where, own, oth, left, right):
-    c = where[2]
+    c, m = where[2], where[3]
 
     def step(k, carry):
         z, shift = k // NX, k % NX
-        xp = shift_of(where, shift)
-        start = xp * (NZ * NC * B) + z * (NC * B)
+        start = shift_of(where, shift) * (NZ * NC * B) + z * (NC * B)
         for ref, core in ((own, c), (oth, 1 - c)):
             row = pl.multiple_of(start + core * B, B)
-            for arr, out in ((0, left), (1, right)):
-                for m in range(NM):
-                    out[pl.ds(row, B), m * W : (m + 1) * W] = ref[m, z, arr * NX + shift]
+            for t in range(NM):
+                col = block_start(lax.rem(m - t + NM, NM), W)
+                left[pl.ds(row, B), pl.ds(col, W)] = ref[z, 2 * NX * t + shift]
+                right[pl.ds(row, B), pl.ds(col, W)] = ref[z, 2 * NX * t + NX + shift]
         return carry
 
     lax.fori_loop(0, NZ * NX, step, 0)
 
 
-def old_power_kernel(where, pack, from1, from3, from2, left, right, out, block):
+def old_power_kernel(where, pack, left, right, out, block):
     c, m = where[2], where[3]
 
     def fill(n, piece):
@@ -133,10 +162,10 @@
 
     for u in range(NM):
         shift = shift_of(where, lax.rem(m + u, NM))
-        fill(u, lambda z, k: pack[z, 16 + NX * k + shift])
-    for n, ref in enumerate((from1, from3, from2)):
+        fill(u, lambda z, k: pack[z, NX * k + shift])
+    for n in range(3):
         for j in range(2):
-            fill(4 + 2 * n + j, lambda z, k: ref[z, 2 * k + j])
+            fill(4 + 2 * n + j, lambda z, k: pack[z, 8 + 4 * n + 2 * k + j])
     table = (
         ((0, 0), (1, 1), (2, 1), (3, 1)),
         ((1, 0), (6, 0), (7, 1), (5, 0)),
@@ -201,8 +230,8 @@
     def step(k, carry):
         xp, zp = k // NZ, k % NZ
         value = rot[pl.ds(pl.multiple_of(k * (NC * B) + c * B, B), B), :]
-        one = 0.9 * pack[zp, 2 * NX + shift_of(where, xp)].astype(F32) + 0.1 * value
-        two = 0.95 * pack[zp, 3 * NX + shift_of(where, xp)].astype(F32) + 0.05 * value * value
+        one = 0.9 * pack[zp, 8 * NX + shift_of(where, xp)].astype(F32) + 0.1 * value
+        two = 0.95 * pack[zp, 9 * NX + shift_of(where, xp)].astype(F32) + 0.05 * value * value
         value = (one / FIX_ONE / (jnp.sqrt(two / FIX_TWO) + 1e-08)).astype(BF)
         for copy in range(NM):
             direct[copy, pl.ds(block_start(k, B), B), :] = value
@@ -392,11 +421,6 @@
         rows = [home[0]] + [
             lax.ppermute(home[s], "x", [(i, (i + s) % NX) for i in range(NX)]) for s in (1, 2, 3)
         ]
-        stats_recv = swap_cores(jnp.stack([r[5] for r in rows]))
-        pack = jnp.stack([r[:5] for r in rows], axis=1).reshape(5 * NX, B, W)
-        pack = jnp.concatenate([pack, stats_recv], axis=0)
-        pack = lax.all_gather(pack, "z", axis=0)
-
     with jax.named_scope("grad_sum"):
         feat_other = lax.dynamic_slice_in_dim(features, (1 - ci) * half, half, 1)
         feat_mine = lax.dynamic_slice_in_dim(features, ci * half, half, 1)
@@ -410,37 +434,33 @@
 
         grads_o, norm_o = partial(feat_other, 1 - ci)
         sent = jnp.concatenate([grads_o.astype(BF), norm_o.astype(BF)], axis=1)
+        *rows, sent = lax.optimization_barrier((*rows, sent))
         got = swap_cores(sent)
+        stats_recv = swap_cores(jnp.stack([r[5] for r in rows]))
+        rows_of_z = lambda n: jax.ShapeDtypeStruct((n, B, W), BF)
+        bases, moments, stats, near, far = pl.pallas_call(
+            spread_kernel,
+            out_shape=[rows_of_z(n) for n in (8, 8, 8, 4, 4)],
+            in_specs=[VMEM] * 5,
+            out_specs=[VMEM] * 5,
+            name="spread",
+        )(*rows, stats_recv)
+        turned = [turn(bases, s) for s in (1, 2, 3)]
         grads_s, norm_s = partial(feat_mine, ci)
         acc = jnp.concatenate([grads_s, norm_s], axis=1) + got.astype(F32)
-        acc = exchange(acc.astype(BF), "x")
+        acc, *turned = lax.optimization_barrier((acc.astype(BF), *turned))
+        pack = lax.all_gather(join(bases, *turned, moments), "z", axis=0)
+        acc = exchange(acc, "x")
+        stats = join(stats, turn(far, 1), turn(near, 3), turn(near, 2))
 
     with jax.named_scope("grad_sum"):
         acc = jnp.sum(acc.astype(F32), axis=0)
         norm_z = jnp.pad(acc[half].reshape(NZ, 1, 32), ((0, 0), (0, PAD - 1), (0, W - 32)))
         acc = jnp.concatenate([acc[:half].reshape(NZ, half // NZ, W), norm_z], axis=1)
         acc = exchange(acc.astype(BF), "z")
-        acc, pack = lax.optimization_barrier((acc, pack))
         acc = jnp.sum(acc.astype(F32), axis=0)
         grad_rows = acc[: half // NZ].astype(BF)
         norm_total = acc[half // NZ, :32]
-
-    with jax.named_scope("state_all"):
-        piece = (NZ, 4, B, W)
-        bases, near, far = call(
-            select_kernel,
-            "select",
-            [((NZ, 8, B, W), BF), (piece, BF), (piece, BF)],
-            [],
-            where,
-            pack,
-        )
-        bases = lax.all_gather(bases, "mp", axis=0)
-
-        def turn(value, s):
-            return lax.ppermute(value, "mp", [(i, (i + s) % NM) for i in range(NM)])
-
-        stats = [turn(far, 1), turn(near, 3), turn(near, 2)]
 
     new_nm = 0.9 * norm_m + 0.1 * norm_total
     new_nv = 0.95 * norm_v + 0.05 * norm_total * norm_total
@@ -452,14 +472,22 @@
         norm_zs = grad_z[:, half // NZ, None, :32]
         norm_zs = jnp.where(jnp.arange(NC)[None, :, None] == ci, norm_zs, 0).reshape(2, W)
         grad_half = grad_z[:, : half // NZ].reshape(half, W)
-        grad_half, *stats = lax.optimization_barrier((grad_half, *stats))
+        pack, norm_zs, stats = lax.optimization_barrier((pack, norm_zs, stats))
+        stats = lax.all_gather(stats, "z", axis=0)
+        pack_other = swap_cores(pack)
+        left, right = call(
+            prep_kernel,
+            "prep",
+            [((full, full), BF)] * 2,
+            [],
+            where,
+            pack,
+            pack_other,
+            cost=COST,
+        )
         grad_half = everyone(grad_half, "mp", NM)
-        grad_half, bases = lax.optimization_barrier((grad_half, bases))
+        grad_half, left, right = lax.optimization_barrier((grad_half, left, right))
         grad_other = swap_cores(grad_half)
-        bases_other = swap_cores(bases)
-        left, right = call(
-            prep_kernel, "prep", [((full, full), BF)] * 2, [], where, bases, bases_other
-        )
 
     with jax.named_scope("rotate"):
         grad, work, direction, rot_home = call(
@@ -479,6 +507,7 @@
             right,
             pack,
         )
+        stats, rot_home = lax.optimization_barrier((stats, rot_home))
         direction = exchange(direction, "mp")
     with jax.named_scope("power"):
         (power_old,) = call(
@@ -487,8 +516,7 @@
             [((full, full), F32)],
             [((10, W, W), BF)],
             where,
-            pack,
-            *stats,
+            stats,
             left,
             right,
             cost=COST,

time: 212 us -> 196 us (0.925)
  waiting for transfers between devices: 30.8 us -> 15.3 us
  local copies, waits for them, and re-layouts: 24.3 us -> 19.4 us
  Pallas kernels: 35.6 us -> 38.5 us
    all_to_all x3, waiting for transfers between devices: 14.5 us -> 6.01 us  [exchange(): return lax.all_to_all(value, axis, 0, 0, tiled=True)]
    unnamed x61 -> x65, local copies, waits for them, and re-layouts: 19.3 us -> 14.4 us
    pallas_call x0 -> x3, Pallas kernels: none -> 4.82 us  [the longest x2 3.26 us: join(): pl.pallas_call(join_kernel, out_shape=jax.ShapeDtypeStruct(shape, parts[0...]
    all_to_all x3, starting transfers between devices: 15.4 us -> 10.6 us  [exchange(): return lax.all_to_all(value, axis, 0, 0, tiled=True)]
    ppermute x6, waiting for transfers between devices: 9.38 us -> 5.07 us  [swap_cores(): return lax.ppermute(value, 'c', [(0, 1), (1, 0)])]
    ppermute x3 -> x6, waiting for transfers between devices: 6.88 us -> 4.16 us  [turn(): return lax.ppermute(value, 'mp', [(i, (i + s) % NM) for i in range(NM)])]
    ppermute x6, starting transfers between devices: 6.69 us -> 8.84 us  [swap_cores(): return lax.ppermute(value, 'c', [(0, 1), (1, 0)])]
    pallas_call x9 -> x8, Pallas kernels: 33.7 us -> 31.8 us  [call(): pl.pallas_call(kernel, out_shape=[jax.ShapeDtypeStruct(s, d) for s, d in...]
  transfers between devices with their start and end apart: 17 -> 20, of which waited for: 8 -> 7; matrix products, arithmetic and copies ran while one was open for 8% -> 10% of each run, Pallas kernels for 8% -> 16%
where the time goes in v2:
time: 196 us; the launch traced here: 195 us
  blocking collectives  59.7 us (30%)
  Pallas kernels  38.5 us (20%)
  starting transfers between devices  32.3 us (16%)
  local copies, waits for them, and re-layouts  19.4 us (10%)
  between operations  16.4 us (8%)
  waiting for transfers between devices  15.3 us (8%)
  other arithmetic  7.06 us (4%)
  matrix products  6.35 us (3%)
    all_to_all x3, blocking collectives, exchange(): return lax.all_to_all(value, axis, 0, 0, tiled=True)  59.7 us
    pallas_call x8, Pallas kernels, call(): pl.pallas_call(kernel, out_shape=[jax.ShapeDtypeStruct(s, d) for s, d in...  31.8 us
    unnamed x65, local copies, waits for them, and re-layouts  14.4 us
    all_to_all x3, starting transfers between devices, exchange(): return lax.all_to_all(value, axis, 0, 0, tiled=True)  10.6 us
    ppermute x6, starting transfers between devices, swap_cores(): return lax.ppermute(value, 'c', [(0, 1), (1, 0)])  8.84 us
    ppermute x6, starting transfers between devices, turn(): return lax.ppermute(value, 'mp', [(i, (i + s) % NM) for i in range(NM)])  7 us
    dot_general x2, matrix products, partial(): jnp.einsum('ti,tnc->nic', feat, out_grads, preferred_element_type=F32)  6.35 us
    all_to_all x3, waiting for transfers between devices, exchange(): return lax.all_to_all(value, axis, 0, 0, tiled=True)  6.01 us
  transfers between devices with their start and end apart: 20, of which 7 were waited for; matrix products, arithmetic and copies ran while one was open for 10% of the time, Pallas kernels for 16%

profile of v2, /device:TPU:1, one launch (start us, length us, event | category | flops | bytes accessed | tf_op | source)
XLA Modules:
  0.0 195.0 jit_solution(2116017005912920942)
XLA Ops:
  7.2 1.9 pack.1
  9.1 2.1 %collective-permute-start = (bf16[6,16,256]{2,1,0:T(8,128)(2,1)}, bf16[6,16,256]{2,1,0:T(8,128)(2,1)S(1)}, u32[]{:S(2)}, u32[]{:S(2)}) collective-permute-start(bf16[6,16,256]{2,1,0:T(8,128)(2,1)} %get-tuple-element.58), channel_id=1, source_target_pairs={{0,64},{64,128},{128,192},{192,0},{1,65},{65,129},{129,193},{193,1... | collective-permute-start | bytes 147464 | tf_op jit(solution)/shard_map/state_rows/ppermute | solution.py:422
  11.2 2.5 %collective-permute-start.1 = (bf16[6,16,256]{2,1,0:T(8,128)(2,1)}, bf16[6,16,256]{2,1,0:T(8,128)(2,1)S(1)}, u32[]{:S(2)}, u32[]{:S(2)}) collective-permute-start(bf16[6,16,256]{2,1,0:T(8,128)(2,1)} %get-tuple-element.59), channel_id=1, source_target_pairs={{0,128},{64,192},{128,0},{192,64},{1,129},{65,193},{129,1},{193,65... | collective-permute-start | bytes 147464 | tf_op jit(solution)/shard_map/state_rows/ppermute | solution.py:422
  13.7 1.2 collective-permute-start.2
  14.8 0.5 broadcast.43
  15.4 1.4 reduce.6
  17.0 2.5 %fusion.13 = bf16[4,512,256]{2,1,0:T(8,128)(2,1)S(1)} fusion(bf16[1024,4,256]{2,1,0:T(4,128)(2,1)S(1)} %copy-done, bf16[1024,1024]{1,0:T(8,128)(2,1)} %param.12, s32[]{:T(128)S(6)} %select_n.32), kind=kOutput, calls=%fused_computation.11 | convolution fusion | flops 1074266112 | bytes 4194308 | tf_op jit(solution)/shard_map/grad_sum/ti,tnc->nic/dot_general | solution.py:430
  19.6 1.6 collective-permute-start.3
  21.2 0.7 slice.41
  22.1 3.9 %fusion.7 = f32[4,512,256]{2,1,0:T(8,128)} fusion(bf16[1024,4,256]{2,1,0:T(4,128)(2,1)S(1)} %copy-done, bf16[1024,1024]{1,0:T(8,128)(2,1)} %param.12, s32[]{:T(128)S(6)} %select_n.30), kind=kOutput, calls=%fused_computation.9 | convolution fusion | flops 1073741824 | bytes 5242884 | tf_op jit(solution)/shard_map/grad_sum/ti,tnc->nic/dot_general | solution.py:430
  26.0 0.6 copy-done.24
  26.6 1.6 spread.1
  28.2 1.3 collective-permute-start.5
  29.5 2.6 %collective-permute-start.6 = (bf16[8,16,256]{2,1,0:T(8,128)(2,1)}, bf16[8,16,256]{2,1,0:T(8,128)(2,1)S(1)}, u32[]{:S(2)}, u32[]{:S(2)}) collective-permute-start(bf16[8,16,256]{2,1,0:T(8,128)(2,1)} %get-tuple-element.66.refs_0_), channel_id=1, source_target_pairs={{0,2},{1,3},{2,0},{3,1},{4,6},{5,7},{6,4},{7,5},{8,10},{9,11},{10,... | collective-permute-start | bytes 196616 | tf_op jit(solution)/shard_map/grad_sum/ppermute | solution.py:33
  32.1 1.1 collective-permute-start.7
  33.1 2.1 %fusion.1 = bf16[4,528,256]{2,1,0:T(8,128)(2,1)S(1)} fusion(f32[4,1,256]{2,1,0:T(1,128)S(1)} %reshape.49, f32[4,512,256]{2,1,0:T(8,128)} %fusion.7, bf16[4,528,256]{2,1,0:T(8,128)(2,1)} %collective-permute-done.3), kind=kLoop, calls=%fused_computation.2 | loop fusion | flops 3244032 | bytes 4263936 | tf_op jit(solution)/shard_map/grad_sum/convert_element_type | solution.py:451
  35.3 0.4 collective-permute-done.7.refs_3_
  35.9 0.4 copy-done.21
  36.3 1.7 join.2
  38.1 16.7 %all_to_all.30 = bf16[4,528,256]{2,1,0:T(8,128)(2,1)} all-to-all(bf16[4,528,256]{2,1,0:T(8,128)(2,1)S(1)} %fusion.1), channel_id=1, replica_groups=mesh['x'=4,'z'=8,'c'=2,'mp'=4] {'x'}, dimensions={0} | all-to-all | bytes 2162688 | tf_op jit(solution)/shard_map/grad_sum/all_to_all | solution.py:29
  54.8 1.5 reduce
  56.5 23.2 %all_to_all.31 = bf16[8,80,256]{2,1,0:T(8,128)(2,1)S(1)} all-to-all(bf16[8,80,256]{2,1,0:T(8,128)(2,1)S(1)} %fusion.22), channel_id=1, replica_groups=mesh['x'=4,'z'=8,'c'=2,'mp'=4] {'z'}, dimensions={0} | all-to-all | bytes 655360 | tf_op jit(solution)/shard_map/grad_sum/all_to_all | solution.py:29
  79.8 0.5 convert_bitcast_fusion
  80.4 0.7 broadcast_in_dim.46
  81.1 3.4 %all-to-all-start.2 = ((bf16[8,80,256]{2,1,0:T(8,128)(2,1)}), bf16[8,80,256]{2,1,0:T(8,128)(2,1)S(1)}, u32[]{:S(2)}, u32[]{:S(2)}) async-start(bf16[8,80,256]{2,1,0:T(8,128)(2,1)} %broadcast_in_dim.46), calls=%async_computation.2 | async-start | bytes 655360 | tf_op jit(solution)/shard_map/grad_all/all_to_all | solution.py:29
  84.6 1.2 collective-permute-start.9
  85.8 0.4 collective-permute-start.10
  86.2 0.5 collective-permute-start.8
  86.6 3.8 %collective-permute-done.8.refs_1_ = bf16[4,16,256]{2,1,0:T(8,128)(2,1)S(1)} collective-permute-done((bf16[4,16,256]{2,1,0:T(8,128)(2,1)S(1)}, bf16[4,16,256]{2,1,0:T(8,128)(2,1)S(1)}, u32[]{:S(2)}, u32[]{:S(2)}) %collective-permute-start.8) | collective-permute-done | bytes 32800 | tf_op jit(solution)/shard_map/grad_sum/ppermute | solution.py:33
  90.4 0.6 copy-done.25
  91.0 1.5 join.3
  92.6 2.0 %all-to-all-done.2 = bf16[8,80,256]{2,1,0:T(8,128)(2,1)S(1)} async-done(((bf16[8,80,256]{2,1,0:T(8,128)(2,1)}), bf16[8,80,256]{2,1,0:T(8,128)(2,1)S(1)}, u32[]{:S(2)}, u32[]{:S(2)}) %all-to-all-start.2) | async-done | bytes 327712 | tf_op jit(solution)/shard_map/grad_all/all_to_all | solution.py:29
  94.8 5.2 %collective-permute-start.11 = (bf16[8,40,16,256]{3,2,1,0:T(8,128)(2,1)}, bf16[8,40,16,256]{3,2,1,0:T(8,128)(2,1)}, u32[]{:S(2)}, u32[]{:S(2)}) collective-permute-start(bf16[8,40,16,256]{3,2,1,0:T(8,128)(2,1)} %bitcast.54), channel_id=1, source_target_pairs={{0,4},{4,0},{1,5},{5,1},{2,6},{6,2},{3,7},{7,3},{8,12},{12,8},{9,1... | collective-permute-start | bytes 7864328 | tf_op jit(solution)/shard_map/grad_all/ppermute | solution.py:25
  100.0 0.6 slice.40
  100.6 1.0 broadcast_in_dim.48
  101.7 3.7 %all-to-all-start.3 = ((bf16[4,512,256]{2,1,0:T(8,128)(2,1)}), bf16[4,512,256]{2,1,0:T(8,128)(2,1)S(1)}, u32[]{:S(2)}, u32[]{:S(2)}) async-start(bf16[4,512,256]{2,1,0:T(8,128)(2,1)} %broadcast_in_dim.48), calls=%async_computation.3 | async-start | bytes 2097152 | tf_op jit(solution)/shard_map/grad_all/all_to_all | solution.py:29
  105.4 0.6 compare_reduce_fusion
  108.0 0.6 fusion.29
  108.6 1.4 stack.54.where
  110.0 3.7 %prep.1 = (bf16[1024,1024]{1,0:T(8,128)(2,1)S(1)}, bf16[1024,1024]{1,0:T(8,128)(2,1)S(1)}) custom-call(s32[9]{0:T(128)S(1)} %stack.54.where, bf16[8,40,16,256]{3,2,1,0:T(8,128)(2,1)} %bitcast.55, bf16[8,40,16,256]{3,2,1,0:T(8,128)(2,1)} %collective-permute-done.11.oth), custom_call_target="tpu_custom_call" | custom-call | flops 6000000000 | bytes 24000000 | tf_op jit(solution)/shard_map/grad_all/prep/pallas_call | solution.py:65
  113.7 1.4 copy-done.1
  115.0 1.4 copy-done.4
  116.4 4.0 %all-to-all-done.3.own = bf16[4,512,256]{2,1,0:T(8,128)(2,1)S(1)} async-done(((bf16[4,512,256]{2,1,0:T(8,128)(2,1)}), bf16[4,512,256]{2,1,0:T(8,128)(2,1)S(1)}, u32[]{:S(2)}, u32[]{:S(2)}) %all-to-all-start.3) | async-done | bytes 1048608 | tf_op jit(solution)/shard_map/grad_all/all_to_all | solution.py:29
  120.4 0.8 collective-permute-start.12
  121.2 2.3 %collective-permute-done.12.oth = bf16[4,512,256]{2,1,0:T(8,128)(2,1)S(1)} collective-permute-done((bf16[4,512,256]{2,1,0:T(8,128)(2,1)S(1)}, bf16[4,512,256]{2,1,0:T(8,128)(2,1)S(1)}, u32[]{:S(2)}, u32[]{:S(2)}) %collective-permute-start.12) | collective-permute-done | bytes 1048608 | tf_op jit(solution)/shard_map/grad_all/ppermute | solution.py:25
  123.5 10.2 %rotate.1 = (bf16[1024,1024]{1,0:T(8,128)(2,1)S(1)}, bf16[1024,1024]{1,0:T(8,128)(2,1)}, bf16[4,512,256]{2,1,0:T(8,128)(2,1)S(1)}, bf16[4,16,256]{2,1,0:T(8,128)(2,1)S(1)}) custom-call(s32[9]{0:T(128)S(1)} %stack.54.where, bf16[4,512,256]{2,1,0:T(8,128)(2,1)S(1)} %all-to-all-done.3.own, bf16[4,512,256]{2,1,0:T(8,128)(2,1)S(1)} %collective-permute-done.12.oth, ...), custom_call_target="tpu_custom_call" | custom-call | tf_op jit(solution)/shard_map/rotate/rotate/pallas_call | solution.py:65
  133.7 1.0 copy-done.7
  134.6 1.4 copy-done.12
  136.0 3.5 %all-to-all-start.4 = ((bf16[4,512,256]{2,1,0:T(8,128)(2,1)}), bf16[4,512,256]{2,1,0:T(8,128)(2,1)S(1)}, u32[]{:S(2)}, u32[]{:S(2)}) async-start(bf16[4,512,256]{2,1,0:T(8,128)(2,1)} %copy-done.7), calls=%async_computation.4 | async-start | bytes 2097152 | tf_op jit(solution)/shard_map/rotate/all_to_all | solution.py:29
  139.6 1.6 copy-done.2
  141.2 1.6 copy-done.5
  142.8 1.3 copy-done.15
  144.1 5.0 %old_power.1.old = f32[1024,1024]{1,0:T(8,128)} custom-call(s32[9]{0:T(128)S(1)} %stack.54.where, bf16[8,20,16,256]{3,2,1,0:T(8,128)(2,1)S(1)} %bitcast.53, bf16[1024,1024]{1,0:T(8,128)(2,1)S(1)} %copy-done.2, bf16[1024,1024]{1,0:T(8,128)(2,1)S(1)} %copy-done.5), custom_call_target="tpu_custom_call" | custom-call | flops 6000000000 | bytes 24000000 | tf_op jit(solution)/shard_map/power/old_power/pallas_call | solution.py:65
  149.1 8.6 %power.1 = (bf16[4,32,256]{2,1,0:T(8,128)(2,1)S(1)}, bf16[4,32,256]{2,1,0:T(8,128)(2,1)S(1)}) custom-call(s32[9]{0:T(128)S(1)} %stack.54.where, bf16[1024,1024]{1,0:T(8,128)(2,1)S(1)} %copy-done.13, bf16[1024,1024]{1,0:T(8,128)(2,1)S(1)} %copy-done.14, f32[1024,1024]{1,0:T(8,128)} %old_power.1.old), custom_call_target="tpu_custom_call" | custom-call | flops 6000000000 | bytes 24000000 | tf_op jit(solution)/shard_map/power/power/pallas_call | solution.py:65
  157.7 1.7 copy-done.6
  159.4 1.0 back.1.own
  160.5 1.5 collective-permute-done.13.oth
  162.1 1.2 update.1
  163.4 19.8 %all_to_all.32.got = bf16[4,608,256]{2,1,0:T(8,128)(2,1)S(1)} all-to-all(bf16[4,608,256]{2,1,0:T(8,128)(2,1)S(1)} %update.1), channel_id=1, replica_groups=mesh['x'=4,'z'=8,'c'=2,'mp'=4] {'x'}, dimensions={0} | all-to-all | bytes 2490368 | tf_op jit(solution)/shard_map/home/all_to_all | solution.py:29
  183.1 0.6 relay.1
  183.8 1.0 collective-permute-start.14
  184.8 1.3 collective-permute-done.14.recv
  186.1 1.5 final.1
  187.6 0.6 copy.79
  (94 shorter events, 1.5 us)
Async XLA Ops:
  7.2 9.8 %copy-start = (bf16[1024,4,256]{2,1,0:T(4,128)(2,1)S(1)}, bf16[1024,4,256]{2,1,0:T(4,128)(2,1)}, u32[]{:S(2)}) copy-start(bf16[1024,4,256]{2,1,0:T(4,128)(2,1)} %param.13) | copy-start | bytes 6291460
  7.2 87.6 %all-gather.5.cloned.1.call-start = ((), (), s32[]{:S(2)}) async-start(), calls=%async_computation.6 | async-start | bytes 2949120 | tf_op jit(solution)/shard_map/grad_sum/all_gather | solution.py:452
  9.1 10.4 %collective-permute-start = (bf16[6,16,256]{2,1,0:T(8,128)(2,1)}, bf16[6,16,256]{2,1,0:T(8,128)(2,1)S(1)}, u32[]{:S(2)}, u32[]{:S(2)}) collective-permute-start(bf16[6,16,256]{2,1,0:T(8,128)(2,1)} %get-tuple-element.58), channel_id=1, source_target_pairs={{0,64},{64,128},{128,192},{192,0},{1,65},{65,129},{129,193},{193,1... | collective-permute-start | bytes 147464 | tf_op jit(solution)/shard_map/state_rows/ppermute | solution.py:422
  11.2 8.3 %collective-permute-start.1 = (bf16[6,16,256]{2,1,0:T(8,128)(2,1)}, bf16[6,16,256]{2,1,0:T(8,128)(2,1)S(1)}, u32[]{:S(2)}, u32[]{:S(2)}) collective-permute-start(bf16[6,16,256]{2,1,0:T(8,128)(2,1)} %get-tuple-element.59), channel_id=1, source_target_pairs={{0,128},{64,192},{128,0},{192,64},{1,129},{65,193},{129,1},{193,65... | collective-permute-start | bytes 147464 | tf_op jit(solution)/shard_map/state_rows/ppermute | solution.py:422
  13.7 5.9 %collective-permute-start.2 = (bf16[6,16,256]{2,1,0:T(8,128)(2,1)}, bf16[6,16,256]{2,1,0:T(8,128)(2,1)S(1)}, u32[]{:S(2)}, u32[]{:S(2)}) collective-permute-start(bf16[6,16,256]{2,1,0:T(8,128)(2,1)} %get-tuple-element.60), channel_id=1, source_target_pairs={{0,192},{64,0},{128,64},{192,128},{1,193},{65,1},{129,65},{193,129... | collective-permute-start | bytes 147464 | tf_op jit(solution)/shard_map/state_rows/ppermute | solution.py:422
  19.6 6.4 %copy-start.16 = (bf16[6,16,256]{2,1,0:T(8,128)(2,1)}, bf16[6,16,256]{2,1,0:T(8,128)(2,1)S(1)}, u32[]{:S(2)}) copy-start(bf16[6,16,256]{2,1,0:T(8,128)(2,1)S(1)} %collective-permute-done.r1) | copy-start | bytes 147460
  19.6 6.3 %copy-start.17 = (bf16[6,16,256]{2,1,0:T(8,128)(2,1)}, bf16[6,16,256]{2,1,0:T(8,128)(2,1)S(1)}, u32[]{:S(2)}) copy-start(bf16[6,16,256]{2,1,0:T(8,128)(2,1)S(1)} %collective-permute-done.1.r2) | copy-start | bytes 147460
  19.6 6.3 %copy-start.18 = (bf16[6,16,256]{2,1,0:T(8,128)(2,1)}, bf16[6,16,256]{2,1,0:T(8,128)(2,1)S(1)}, u32[]{:S(2)}) copy-start(bf16[6,16,256]{2,1,0:T(8,128)(2,1)S(1)} %collective-permute-done.2.r3) | copy-start | bytes 147460
  19.6 13.5 %collective-permute-start.3 = (bf16[4,528,256]{2,1,0:T(8,128)(2,1)S(1)}, bf16[4,528,256]{2,1,0:T(8,128)(2,1)}, u32[]{:S(2)}, u32[]{:S(2)}) collective-permute-start(bf16[4,528,256]{2,1,0:T(8,128)(2,1)S(1)} %fusion.16), channel_id=1, source_target_pairs={{0,4},{4,0},{1,5},{5,1},{2,6},{6,2},{3,7},{7,3},{8,12},{12,8},{9,1... | collective-permute-start | bytes 3244040 | tf_op jit(solution)/shard_map/grad_sum/ppermute | solution.py:25
  21.9 4.1 %collective-permute-start.4 = (bf16[4,16,256]{2,1,0:T(8,128)(2,1)S(1)}, bf16[4,16,256]{2,1,0:T(8,128)(2,1)S(1)}, u32[]{:S(2)}, u32[]{:S(2)}) collective-permute-start(bf16[4,16,256]{2,1,0:T(8,128)(2,1)S(1)} %pad_maximum_fusion), channel_id=1, source_target_pairs={{0,4},{4,0},{1,5},{5,1},{2,6},{6,2},{3,7},{7,3},{8,12},{12,8},{9,1... | collective-permute-start | bytes 98312 | tf_op jit(solution)/shard_map/grad_sum/ppermute | solution.py:25
  26.0 0.6 copy-start.24
  28.2 7.1 %collective-permute-start.5 = (bf16[8,16,256]{2,1,0:T(8,128)(2,1)}, bf16[8,16,256]{2,1,0:T(8,128)(2,1)S(1)}, u32[]{:S(2)}, u32[]{:S(2)}) collective-permute-start(bf16[8,16,256]{2,1,0:T(8,128)(2,1)} %get-tuple-element.66.refs_0_), channel_id=1, source_target_pairs={{0,1},{1,2},{2,3},{3,0},{4,5},{5,6},{6,7},{7,4},{8,9},{9,10},{10,1... | collective-permute-start | bytes 196616 | tf_op jit(solution)/shard_map/grad_sum/ppermute | solution.py:33
  29.5 5.8 %collective-permute-start.6 = (bf16[8,16,256]{2,1,0:T(8,128)(2,1)}, bf16[8,16,256]{2,1,0:T(8,128)(2,1)S(1)}, u32[]{:S(2)}, u32[]{:S(2)}) collective-permute-start(bf16[8,16,256]{2,1,0:T(8,128)(2,1)} %get-tuple-element.66.refs_0_), channel_id=1, source_target_pairs={{0,2},{1,3},{2,0},{3,1},{4,6},{5,7},{6,4},{7,5},{8,10},{9,11},{10,... | collective-permute-start | bytes 196616 | tf_op jit(solution)/shard_map/grad_sum/ppermute | solution.py:33
  32.1 3.6 %collective-permute-start.7 = (bf16[8,16,256]{2,1,0:T(8,128)(2,1)}, bf16[8,16,256]{2,1,0:T(8,128)(2,1)S(1)}, u32[]{:S(2)}, u32[]{:S(2)}) collective-permute-start(bf16[8,16,256]{2,1,0:T(8,128)(2,1)} %get-tuple-element.66.refs_0_), channel_id=1, source_target_pairs={{0,3},{1,0},{2,1},{3,2},{4,7},{5,4},{6,5},{7,6},{8,11},{9,8},{10,9... | collective-permute-start | bytes 196616 | tf_op jit(solution)/shard_map/grad_sum/ppermute | solution.py:33
  35.3 0.6 copy-start.19
  35.3 0.6 copy-start.20
  35.7 0.6 copy-start.21
  54.8 25.0 %copy-start.27 = (f32[32]{0:T(128)S(1)}, f32[32]{0:T(128)}, u32[]{:S(2)}) copy-start(f32[32]{0:T(128)} %param.22) | copy-start | bytes 388
  54.8 25.0 %copy-start.28 = (f32[32]{0:T(128)S(1)}, f32[32]{0:T(128)}, u32[]{:S(2)}) copy-start(f32[32]{0:T(128)} %param.23) | copy-start | bytes 388
  54.8 29.8 %copy-start.29 = (bf16[4,16,256]{2,1,0:T(8,128)(2,1)S(1)}, bf16[4,16,256]{2,1,0:T(8,128)(2,1)}, u32[]{:S(2)}) copy-start(bf16[4,16,256]{2,1,0:T(8,128)(2,1)} %get-tuple-element.74) | copy-start | bytes 98308
  54.8 31.3 %copy-start.30 = (bf16[4,16,256]{2,1,0:T(8,128)(2,1)S(1)}, bf16[4,16,256]{2,1,0:T(8,128)(2,1)}, u32[]{:S(2)}) copy-start(bf16[4,16,256]{2,1,0:T(8,128)(2,1)} %get-tuple-element.73) | copy-start | bytes 98308
  56.4 43.7 %copy-start.26 = (s32[5]{0:T(128)S(1)}, s32[5]{0:T(128)}, u32[]{:S(2)}) copy-start(s32[5]{0:T(128)} %param.15) | copy-start | bytes 64
  81.1 13.5 %all-to-all-start.2 = ((bf16[8,80,256]{2,1,0:T(8,128)(2,1)}), bf16[8,80,256]{2,1,0:T(8,128)(2,1)S(1)}, u32[]{:S(2)}, u32[]{:S(2)}) async-start(bf16[8,80,256]{2,1,0:T(8,128)(2,1)} %broadcast_in_dim.46), calls=%async_computation.2 | async-start | bytes 655360 | tf_op jit(solution)/shard_map/grad_all/all_to_all | solution.py:29
  84.5 55.0 %all-gather.7.cloned.1.call-start = ((), (), s32[]{:S(2)}) async-start(), calls=%async_computation.7 | async-start | bytes 1474560 | tf_op jit(solution)/shard_map/grad_all/all_gather | solution.py:476
  84.6 5.8 %collective-permute-start.9 = (bf16[4,16,256]{2,1,0:T(8,128)(2,1)S(1)}, bf16[4,16,256]{2,1,0:T(8,128)(2,1)S(1)}, u32[]{:S(2)}, u32[]{:S(2)}) collective-permute-start(bf16[4,16,256]{2,1,0:T(8,128)(2,1)S(1)} %copy-done.29), channel_id=1, source_target_pairs={{0,3},{1,0},{2,1},{3,2},{4,7},{5,4},{6,5},{7,6},{8,11},{9,8},{10,9... | collective-permute-start | bytes 98312 | tf_op jit(solution)/shard_map/grad_sum/ppermute | solution.py:33
  85.8 4.6 %collective-permute-start.10 = (bf16[4,16,256]{2,1,0:T(8,128)(2,1)S(1)}, bf16[4,16,256]{2,1,0:T(8,128)(2,1)S(1)}, u32[]{:S(2)}, u32[]{:S(2)}) collective-permute-start(bf16[4,16,256]{2,1,0:T(8,128)(2,1)S(1)} %copy-done.29), channel_id=1, source_target_pairs={{0,2},{1,3},{2,0},{3,1},{4,6},{5,7},{6,4},{7,5},{8,10},{9,11},{10,... | collective-permute-start | bytes 98312 | tf_op jit(solution)/shard_map/grad_sum/ppermute | solution.py:33
  86.2 4.2 %collective-permute-start.8 = (bf16[4,16,256]{2,1,0:T(8,128)(2,1)S(1)}, bf16[4,16,256]{2,1,0:T(8,128)(2,1)S(1)}, u32[]{:S(2)}, u32[]{:S(2)}) collective-permute-start(bf16[4,16,256]{2,1,0:T(8,128)(2,1)S(1)} %copy-done.30), channel_id=1, source_target_pairs={{0,1},{1,2},{2,3},{3,0},{4,5},{5,6},{6,7},{7,4},{8,9},{9,10},{10,1... | collective-permute-start | bytes 98312 | tf_op jit(solution)/shard_map/grad_sum/ppermute | solution.py:33
  90.4 0.6 copy-start.25
  90.4 0.6 copy-start.22
  90.4 0.6 copy-start.23
  94.8 15.2 %collective-permute-start.11 = (bf16[8,40,16,256]{3,2,1,0:T(8,128)(2,1)}, bf16[8,40,16,256]{3,2,1,0:T(8,128)(2,1)}, u32[]{:S(2)}, u32[]{:S(2)}) collective-permute-start(bf16[8,40,16,256]{3,2,1,0:T(8,128)(2,1)} %bitcast.54), channel_id=1, source_target_pairs={{0,4},{4,0},{1,5},{5,1},{2,6},{6,2},{3,7},{7,3},{8,12},{12,8},{9,1... | collective-permute-start | bytes 7864328 | tf_op jit(solution)/shard_map/grad_all/ppermute | solution.py:25
  101.7 18.7 %all-to-all-start.3 = ((bf16[4,512,256]{2,1,0:T(8,128)(2,1)}), bf16[4,512,256]{2,1,0:T(8,128)(2,1)S(1)}, u32[]{:S(2)}, u32[]{:S(2)}) async-start(bf16[4,512,256]{2,1,0:T(8,128)(2,1)} %broadcast_in_dim.48), calls=%async_computation.3 | async-start | bytes 2097152 | tf_op jit(solution)/shard_map/grad_all/all_to_all | solution.py:29
  113.7 1.4 copy-start.1
  115.0 1.4 copy-start.4
  120.4 3.1 %collective-permute-start.12 = (bf16[4,512,256]{2,1,0:T(8,128)(2,1)S(1)}, bf16[4,512,256]{2,1,0:T(8,128)(2,1)S(1)}, u32[]{:S(2)}, u32[]{:S(2)}) collective-permute-start(bf16[4,512,256]{2,1,0:T(8,128)(2,1)S(1)} %all-to-all-done.3.own), channel_id=1, source_target_pairs={{0,4},{4,0},{1,5},{5,1},{2,6},{6,2},{3,7},{7,3},{8,12},{12,8},{9,1... | collective-permute-start | bytes 3145736 | tf_op jit(solution)/shard_map/grad_all/ppermute | solution.py:25
  133.7 1.0 copy-start.7
  134.6 1.4 copy-start.12
  136.0 21.6 %all-to-all-start.4 = ((bf16[4,512,256]{2,1,0:T(8,128)(2,1)}), bf16[4,512,256]{2,1,0:T(8,128)(2,1)S(1)}, u32[]{:S(2)}, u32[]{:S(2)}) async-start(bf16[4,512,256]{2,1,0:T(8,128)(2,1)} %copy-done.7), calls=%async_computation.4 | async-start | bytes 2097152 | tf_op jit(solution)/shard_map/rotate/all_to_all | solution.py:29
  139.6 1.6 copy-start.2
  141.2 1.6 copy-start.5
  142.8 1.3 copy-start.15
  144.1 5.0 %copy-start.13 = (bf16[1024,1024]{1,0:T(8,128)(2,1)S(1)}, bf16[1024,1024]{1,0:T(8,128)(2,1)}, u32[]{:S(2)}) copy-start(bf16[1024,1024]{1,0:T(8,128)(2,1)} %copy-done.12) | copy-start | bytes 6291460
  144.1 5.0 %copy-start.14 = (bf16[1024,1024]{1,0:T(8,128)(2,1)S(1)}, bf16[1024,1024]{1,0:T(8,128)(2,1)}, u32[]{:S(2)}) copy-start(bf16[1024,1024]{1,0:T(8,128)(2,1)} %get-tuple-element.83.work) | copy-start | bytes 6291460
  157.7 4.4 %copy-start.3 = (bf16[1024,1024]{1,0:T(8,128)(2,1)S(1)}, bf16[1024,1024]{1,0:T(8,128)(2,1)}, u32[]{:S(2)}) copy-start(bf16[1024,1024]{1,0:T(8,128)(2,1)} %copy-done.1) | copy-start | bytes 6291460
  157.7 1.7 copy-start.6
  160.4 1.6 collective-permute-start.13
  163.3 22.7 %copy-start.8 = (f32[4,16,256]{2,1,0:T(8,128)S(1)}, f32[4,16,256]{2,1,0:T(8,128)}, u32[]{:S(2)}) copy-start(f32[4,16,256]{2,1,0:T(8,128)} %m1.1) | copy-start | bytes 196612
  163.3 22.7 %copy-start.9 = (f32[4,16,256]{2,1,0:T(8,128)S(1)}, f32[4,16,256]{2,1,0:T(8,128)}, u32[]{:S(2)}) copy-start(f32[4,16,256]{2,1,0:T(8,128)} %m2.1) | copy-start | bytes 196612
  163.3 22.7 %copy-start.10 = (f32[4,16,256]{2,1,0:T(8,128)S(1)}, f32[4,16,256]{2,1,0:T(8,128)}, u32[]{:S(2)}) copy-start(f32[4,16,256]{2,1,0:T(8,128)} %sl.1) | copy-start | bytes 196612
  163.3 22.7 %copy-start.11 = (f32[4,16,256]{2,1,0:T(8,128)S(1)}, f32[4,16,256]{2,1,0:T(8,128)}, u32[]{:S(2)}) copy-start(f32[4,16,256]{2,1,0:T(8,128)} %sr.1) | copy-start | bytes 196612
  183.8 2.3 %collective-permute-start.14 = (bf16[656,256]{1,0:T(8,128)(2,1)S(1)}, bf16[656,256]{1,0:T(8,128)(2,1)S(1)}, u32[]{:S(2)}, u32[]{:S(2)}) collective-permute-start(bf16[656,256]{1,0:T(8,128)(2,1)S(1)} %get-tuple-element.95), channel_id=1, source_target_pairs={{0,4},{4,0},{1,5},{5,1},{2,6},{6,2},{3,7},{7,3},{8,12},{12,8},{9,1... | collective-permute-start | bytes 1007624 | tf_op jit(solution)/shard_map/home/ppermute | solution.py:25
Sparse Core Ops, SparseCore 0:
  38.2 48.0 all-gather.4
  100.1 32.1 all-gather.6

commit v3 on v2

--- a/solution.py
+++ b/solution.py
@@ -68,7 +68,7 @@
         in_specs=[SMEM] * n_scalar + [VMEM] * (len(args) - n_scalar),
         out_specs=[VMEM] * len(outs),
         scratch_shapes=[pltpu.VMEM(s, d) for s, d in scratch],
-        compiler_params=pltpu.CompilerParams(vmem_limit_bytes=48 * 1024 * 1024),
+        compiler_params=pltpu.CompilerParams(vmem_limit_bytes=16 * 1024 * 1024),
         cost_estimate=cost,
         name=name,
     )(*args)
@@ -110,20 +110,34 @@
     )(*parts)
 
 
-def spread_kernel(r0, r1, r2, r3, other, bases, moments, stats, near, far):
-    rows = (r0, r1, r2, r3)
-    x, m = lax.axis_index("x"), lax.axis_index("mp")
-    for s, ref in enumerate(rows):
+def spread_kernel(r0, r1, r2, r3, trigger, bases, moments, keep, send):
+    for s, ref in enumerate((r0, r1, r2, r3)):
         for k in range(2):
             bases[NX * k + s] = ref[k]
             moments[NX * k + s] = ref[2 + k]
-        stats[s] = ref[4]
-        stats[NX + s] = other[s]
+        keep[s] = ref[4]
+        send[s] = ref[5]
+
+
+def choose_kernel(keep, other, trigger, stats, near, far):
+    x, m = lax.axis_index("x"), lax.axis_index("mp")
+    stats[:NX] = keep[...]
+    stats[NX:] = other[...]
     for out, steps in ((near, (0, 1)), (far, (0, 2))):
         for j, step in enumerate(steps):
             shift = lax.rem(x - lax.rem(m + step, NM) + NX, NX)
-            for core in range(NC):
-                out[2 * core + j] = stats[NX * core + shift]
+            out[j] = keep[shift]
+            out[2 + j] = other[shift]
+
+
+def small(kernel, name, counts, *args):
+    return pl.pallas_call(
+        kernel,
+        out_shape=[jax.ShapeDtypeStruct((n, B, W), BF) for n in counts],
+        in_specs=[VMEM] * (len(args) - 1) + [pl.BlockSpec(memory_space=pl.ANY)],
+        out_specs=[VMEM] * len(counts),
+        name=name,
+    )(*args)
 
 
 def block_start(index, size):
@@ -136,19 +150,15 @@
 
 def prep_kernel(where, own, oth, left, right):
     c, m = where[2], where[3]
-
-    def step(k, carry):
-        z, shift = k // NX, k % NX
-        start = shift_of(where, shift) * (NZ * NC * B) + z * (NC * B)
-        for ref, core in ((own, c), (oth, 1 - c)):
-            row = pl.multiple_of(start + core * B, B)
-            for t in range(NM):
-                col = block_start(lax.rem(m - t + NM, NM), W)
-                left[pl.ds(row, B), pl.ds(col, W)] = ref[z, 2 * NX * t + shift]
-                right[pl.ds(row, B), pl.ds(col, W)] = ref[z, 2 * NX * t + NX + shift]
-        return carry
-
-    lax.fori_loop(0, NZ * NX, step, 0)
+    for shift in range(NX):
+        start = shift_of(where, shift) * (NZ * NC * B)
+        for t in range(NM):
+            col = block_start(lax.rem(m - t + NM, NM), W)
+            for z in range(NZ):
+                for ref, core in ((own, c), (oth, 1 - c)):
+                    row = pl.multiple_of(start + z * (NC * B) + core * B, B)
+                    left[pl.ds(row, B), pl.ds(col, W)] = ref[z, 2 * NX * t + shift]
+                    right[pl.ds(row, B), pl.ds(col, W)] = ref[z, 2 * NX * t + NX + shift]
 
 
 def old_power_kernel(where, pack, left, right, out, block):
@@ -203,41 +213,24 @@
 
     @pl.when(c == 0)
     def _():
-        def rows(i, carry):
-            r = pl.ds(block_start(i, W), W)
-            work[r, :] = dot_tn(left[:, r], grad[...]).astype(BF)
-            rot[r, :] = dot_nn(work[r, :], right[:, col])
-            return carry
-
-        lax.fori_loop(0, NM, rows, 0)
+        work[...] = dot_tn(left[...], grad[...]).astype(BF)
+        rot[...] = dot_nn(work[...], right[:, col])
 
     @pl.when(c == 1)
     def _():
-        def rows(i, carry):
-            r = pl.ds(block_start(i, W), W)
-            work[r, :] = dot_nn(grad[r, :], right[...]).astype(BF)
-            return carry
-
-        lax.fori_loop(0, NM, rows, 0)
-
-        def more(i, carry):
-            r = pl.ds(block_start(i, W), W)
-            rot[r, :] = dot_tn(left[:, r], work[:, col])
-            return carry
-
-        lax.fori_loop(0, NM, more, 0)
-
-    def step(k, carry):
-        xp, zp = k // NZ, k % NZ
-        value = rot[pl.ds(pl.multiple_of(k * (NC * B) + c * B, B), B), :]
-        one = 0.9 * pack[zp, 8 * NX + shift_of(where, xp)].astype(F32) + 0.1 * value
-        two = 0.95 * pack[zp, 9 * NX + shift_of(where, xp)].astype(F32) + 0.05 * value * value
-        value = (one / FIX_ONE / (jnp.sqrt(two / FIX_TWO) + 1e-08)).astype(BF)
-        for copy in range(NM):
-            direct[copy, pl.ds(block_start(k, B), B), :] = value
-        return carry
-
-    lax.fori_loop(0, NX * NZ, step, 0)
+        work[...] = dot_nn(grad[...], right[...]).astype(BF)
+        rot[...] = dot_tn(left[...], work[:, col])
+
+    for xp in range(NX):
+        shift = shift_of(where, xp)
+        for zp in range(NZ):
+            k = xp * NZ + zp
+            value = rot[pl.ds(pl.multiple_of(k * (NC * B) + c * B, B), B), :]
+            one = 0.9 * pack[zp, 8 * NX + shift].astype(F32) + 0.1 * value
+            two = 0.95 * pack[zp, 9 * NX + shift].astype(F32) + 0.05 * value * value
+            value = (one / FIX_ONE / (jnp.sqrt(two / FIX_TWO) + 1e-08)).astype(BF)
+            for copy in range(NM):
+                direct[copy, k * B : (k + 1) * B, :] = value
     for xp in range(NX):
         row = pl.multiple_of(xp * (NZ * NC * B) + z * (NC * B) + c * B, B)
         rot_home[xp] = rot[pl.ds(row, B), :].astype(BF)
@@ -424,43 +417,36 @@
     with jax.named_scope("grad_sum"):
         feat_other = lax.dynamic_slice_in_dim(features, (1 - ci) * half, half, 1)
         feat_mine = lax.dynamic_slice_in_dim(features, ci * half, half, 1)
-        norm_parts = norm_grads[0].reshape(NX, NZ, NC, 32)
-
-        def partial(feat, core):
-            grads = jnp.einsum("ti,tnc->nic", feat, out_grads, preferred_element_type=F32)
-            norm = lax.dynamic_index_in_dim(norm_parts, core, 2, keepdims=False)
-            norm = jnp.pad(norm.reshape(NX, 1, W), ((0, 0), (0, PAD - 1), (0, 0)))
-            return grads, norm
-
-        grads_o, norm_o = partial(feat_other, 1 - ci)
-        sent = jnp.concatenate([grads_o.astype(BF), norm_o.astype(BF)], axis=1)
+        norm = jnp.pad(norm_grads.reshape(NX, 2, W), ((0, 0), (0, PAD - 2), (0, 0)))
+
+        def partial(feat):
+            return jnp.einsum("ti,tnc->nic", feat, out_grads, preferred_element_type=F32)
+
+        sent = jnp.concatenate([partial(feat_other).astype(BF), norm.astype(BF)], axis=1)
         *rows, sent = lax.optimization_barrier((*rows, sent))
         got = swap_cores(sent)
-        stats_recv = swap_cores(jnp.stack([r[5] for r in rows]))
-        rows_of_z = lambda n: jax.ShapeDtypeStruct((n, B, W), BF)
-        bases, moments, stats, near, far = pl.pallas_call(
-            spread_kernel,
-            out_shape=[rows_of_z(n) for n in (8, 8, 8, 4, 4)],
-            in_specs=[VMEM] * 5,
-            out_specs=[VMEM] * 5,
-            name="spread",
-        )(*rows, stats_recv)
+        acc = jnp.concatenate([partial(feat_mine), norm], axis=1) + got.astype(F32)
+        acc = acc.astype(BF)
+        bases, moments, keep, send = small(spread_kernel, "spread", (8, 8, 4, 4), *rows, acc)
         turned = [turn(bases, s) for s in (1, 2, 3)]
-        grads_s, norm_s = partial(feat_mine, ci)
-        acc = jnp.concatenate([grads_s, norm_s], axis=1) + got.astype(F32)
-        acc, *turned = lax.optimization_barrier((acc.astype(BF), *turned))
         pack = lax.all_gather(join(bases, *turned, moments), "z", axis=0)
-        acc = exchange(acc, "x")
+        tile = lambda s: lax.dynamic_index_in_dim(acc, lax.rem(xi + s, NX), 0, keepdims=False)
+        acc = [tile(0)] + [
+            lax.ppermute(tile(s), "x", [(i, (i + s) % NX) for i in range(NX)]) for s in (2, 1, 3)
+        ]
+
+    with jax.named_scope("grad_sum"):
+        acc = sum(a.astype(F32) for a in acc)
+        norm_z = acc[half : half + 2].reshape(NZ, 1, 64)
+        norm_z = jnp.pad(norm_z, ((0, 0), (0, PAD - 1), (0, W - 64)))
+        acc = jnp.concatenate([acc[:half].reshape(NZ, half // NZ, W), norm_z], axis=1)
+        acc = acc.astype(BF)
+        stats, near, far = small(choose_kernel, "choose", (8, 4, 4), keep, swap_cores(send), acc)
         stats = join(stats, turn(far, 1), turn(near, 3), turn(near, 2))
-
-    with jax.named_scope("grad_sum"):
-        acc = jnp.sum(acc.astype(F32), axis=0)
-        norm_z = jnp.pad(acc[half].reshape(NZ, 1, 32), ((0, 0), (0, PAD - 1), (0, W - 32)))
-        acc = jnp.concatenate([acc[:half].reshape(NZ, half // NZ, W), norm_z], axis=1)
-        acc = exchange(acc.astype(BF), "z")
+        acc = exchange(acc, "z")
         acc = jnp.sum(acc.astype(F32), axis=0)
         grad_rows = acc[: half // NZ].astype(BF)
-        norm_total = acc[half // NZ, :32]
+        norm_total = jnp.where(ci == 0, acc[half // NZ, :32], acc[half // NZ, 32:64])
 
     new_nm = 0.9 * norm_m + 0.1 * norm_total
     new_nv = 0.95 * norm_v + 0.05 * norm_total * norm_total

time: 196 us -> 195 us (level)
  blocking collectives: 59.7 us -> 19.4 us
  waiting for transfers between devices: 15.3 us -> 41.9 us
  starting transfers between devices: 32.3 us -> 45.6 us
  local copies, waits for them, and re-layouts: 19.4 us -> 27.5 us
  Pallas kernels: 38.5 us -> 30.5 us
    all_to_all x3 -> x1, blocking collectives: 59.7 us -> 19.4 us  [exchange(): return lax.all_to_all(value, axis, 0, 0, tiled=True)]
    all_to_all x3 -> x4, waiting for transfers between devices: 6.01 us -> 18.8 us  [exchange(): return lax.all_to_all(value, axis, 0, 0, tiled=True)]
    ppermute x0 -> x3, waiting for transfers between devices: none -> 10.9 us  [shards(): lax.ppermute(tile(s), 'x', [(i, (i + s) % NX) for i in range(NX)])]
    pallas_call x8, Pallas kernels: 31.8 us -> 22.3 us  [call(): pl.pallas_call(kernel, out_shape=[jax.ShapeDtypeStruct(s, d) for s, d in...]
    unnamed x65 -> x75, local copies, waits for them, and re-layouts: 14.4 us -> 22.4 us
    all_to_all x3 -> x4, starting transfers between devices: 10.6 us -> 18.4 us  [exchange(): return lax.all_to_all(value, axis, 0, 0, tiled=True)]
    ppermute x0 -> x3, starting transfers between devices: none -> 2.37 us  [shards(): lax.ppermute(tile(s), 'x', [(i, (i + s) % NX) for i in range(NX)])]
    ppermute x6, waiting for transfers between devices: 4.16 us -> 6.52 us  [turn(): return lax.ppermute(value, 'mp', [(i, (i + s) % NM) for i in range(NM)])]
  transfers between devices with their start and end apart: 20 -> 24, of which waited for: 7 -> 13; matrix products, arithmetic and copies ran while one was open for 10% -> 8% of each run, Pallas kernels for 16% -> 11%
where the time goes in v3:
time: 195 us; the launch traced here: 194 us
  starting transfers between devices  45.6 us (23%)
  waiting for transfers between devices  41.9 us (21%)
  Pallas kernels  30.5 us (16%)
  local copies, waits for them, and re-layouts  27.5 us (14%)
  blocking collectives  19.4 us (10%)
  between operations  16.5 us (8%)
  other arithmetic  7.93 us (4%)
  matrix products  4.99 us (3%)
    unnamed x75, local copies, waits for them, and re-layouts  22.4 us
    pallas_call x8, Pallas kernels, call(): pl.pallas_call(kernel, out_shape=[jax.ShapeDtypeStruct(s, d) for s, d in...  22.3 us
    all_to_all x1, blocking collectives, exchange(): return lax.all_to_all(value, axis, 0, 0, tiled=True)  19.4 us
    all_to_all x4, waiting for transfers between devices, exchange(): return lax.all_to_all(value, axis, 0, 0, tiled=True)  18.8 us
    all_to_all x4, starting transfers between devices, exchange(): return lax.all_to_all(value, axis, 0, 0, tiled=True)  18.4 us
    ppermute x6, starting transfers between devices, swap_cores(): return lax.ppermute(value, 'c', [(0, 1), (1, 0)])  11.1 us
    ppermute x3, waiting for transfers between devices, shards(): lax.ppermute(tile(s), 'x', [(i, (i + s) % NX) for i in range(NX)])  10.9 us
    ppermute x6, starting transfers between devices, turn(): return lax.ppermute(value, 'mp', [(i, (i + s) % NM) for i in range(NM)])  7.92 us
  transfers between devices with their start and end apart: 24, of which 13 were waited for; matrix products, arithmetic and copies ran while one was open for 8% of the time, Pallas kernels for 11%

profile of v3, /device:TPU:1, one launch (start us, length us, event | category | flops | bytes accessed | tf_op | source)
XLA Modules:
  0.0 194.2 jit_solution(13528123343561863060)
XLA Ops:
  7.2 1.9 pack.1
  9.1 2.1 %collective-permute-start = (bf16[6,16,256]{2,1,0:T(8,128)(2,1)}, bf16[6,16,256]{2,1,0:T(8,128)(2,1)S(1)}, u32[]{:S(2)}, u32[]{:S(2)}) collective-permute-start(bf16[6,16,256]{2,1,0:T(8,128)(2,1)} %get-tuple-element.56), channel_id=1, source_target_pairs={{0,64},{64,128},{128,192},{192,0},{1,65},{65,129},{129,193},{193,1... | collective-permute-start | bytes 147464 | tf_op jit(solution)/shard_map/state_rows/ppermute | solution.py:415
  11.2 2.5 %collective-permute-start.1 = (bf16[6,16,256]{2,1,0:T(8,128)(2,1)}, bf16[6,16,256]{2,1,0:T(8,128)(2,1)S(1)}, u32[]{:S(2)}, u32[]{:S(2)}) collective-permute-start(bf16[6,16,256]{2,1,0:T(8,128)(2,1)} %get-tuple-element.57), channel_id=1, source_target_pairs={{0,128},{64,192},{128,0},{192,64},{1,129},{65,193},{129,1},{193,65... | collective-permute-start | bytes 147464 | tf_op jit(solution)/shard_map/state_rows/ppermute | solution.py:415
  13.7 1.2 collective-permute-start.2
  15.4 1.4 reduce.3
  16.8 2.5 %fusion.11 = bf16[4,512,256]{2,1,0:T(8,128)(2,1)S(1)} fusion(bf16[1024,4,256]{2,1,0:T(4,128)(2,1)S(1)} %copy-done, bf16[1024,1024]{1,0:T(8,128)(2,1)} %param.12, s32[]{:T(128)S(6)} %select_n.48), kind=kOutput, calls=%fused_computation.8 | convolution fusion | flops 1074266112 | bytes 4194308 | tf_op jit(solution)/shard_map/grad_sum/ti,tnc->nic/dot_general | solution.py:423
  19.4 1.6 collective-permute-start.3
  21.0 2.5 %fusion.5 = f32[4,512,256]{2,1,0:T(8,128)S(1)} fusion(bf16[1024,4,256]{2,1,0:T(4,128)(2,1)S(1)} %copy-done, bf16[1024,1024]{1,0:T(8,128)(2,1)} %param.12, s32[]{:T(128)S(6)} %select_n.47), kind=kOutput, calls=%fused_computation.6 | convolution fusion | flops 1073741824 | bytes 5242884 | tf_op jit(solution)/shard_map/grad_sum/ti,tnc->nic/dot_general | solution.py:423
  23.6 2.6 %fusion.trigger = bf16[4,528,256]{2,1,0:T(8,128)(2,1)} fusion(f32[4,16,256]{2,1,0:T(8,128)S(1)} %pad.17, f32[4,512,256]{2,1,0:T(8,128)S(1)} %fusion.5, bf16[4,528,256]{2,1,0:T(8,128)(2,1)} %collective-permute-done.3), kind=kLoop, calls=%fused_computation.1 | loop fusion | flops 2162688 | bytes 4325376 | tf_op jit(solution)/shard_map/grad_sum/convert_element_type | solution.py:429
  26.1 1.6 spread.1
  27.7 1.3 collective-permute-start.7
  29.0 2.6 %collective-permute-start.8 = (bf16[8,16,256]{2,1,0:T(8,128)(2,1)}, bf16[8,16,256]{2,1,0:T(8,128)(2,1)S(1)}, u32[]{:S(2)}, u32[]{:S(2)}) collective-permute-start(bf16[8,16,256]{2,1,0:T(8,128)(2,1)} %get-tuple-element.64.refs_0_), channel_id=1, source_target_pairs={{0,2},{1,3},{2,0},{3,1},{4,6},{5,7},{6,4},{7,5},{8,10},{9,11},{10,... | collective-permute-start | bytes 196616 | tf_op jit(solution)/shard_map/grad_sum/ppermute | solution.py:33
  31.7 1.1 collective-permute-start.9
  32.7 2.2 %collective-permute-done.8.refs_2_ = bf16[8,16,256]{2,1,0:T(8,128)(2,1)S(1)} collective-permute-done((bf16[8,16,256]{2,1,0:T(8,128)(2,1)}, bf16[8,16,256]{2,1,0:T(8,128)(2,1)S(1)}, u32[]{:S(2)}, u32[]{:S(2)}) %collective-permute-start.8) | collective-permute-done | bytes 65568 | tf_op jit(solution)/shard_map/grad_sum/ppermute | solution.py:33
  35.9 1.7 join.2
  37.7 0.9 dynamic-slice_bitcast_fusion.2
  39.2 0.9 collective-permute-start.5
  40.1 0.9 collective-permute-start.4
  41.0 4.1 %collective-permute-done.6 = bf16[528,256]{1,0:T(8,128)(2,1)S(1)} collective-permute-done((bf16[528,256]{1,0:T(8,128)(2,1)}, bf16[528,256]{1,0:T(8,128)(2,1)S(1)}, u32[]{:S(2)}, u32[]{:S(2)}) %collective-permute-start.6) | collective-permute-done | bytes 270368 | tf_op jit(solution)/shard_map/grad_sum/ppermute | solution.py:435
  45.1 2.2 %collective-permute-done.5 = bf16[528,256]{1,0:T(8,128)(2,1)} collective-permute-done((bf16[528,256]{1,0:T(8,128)(2,1)}, bf16[528,256]{1,0:T(8,128)(2,1)}, u32[]{:S(2)}, u32[]{:S(2)}) %collective-permute-start.5) | collective-permute-done | bytes 270368 | tf_op jit(solution)/shard_map/grad_sum/ppermute | solution.py:435
  47.3 4.6 %collective-permute-done.4 = bf16[528,256]{1,0:T(8,128)(2,1)} collective-permute-done((bf16[528,256]{1,0:T(8,128)(2,1)}, bf16[528,256]{1,0:T(8,128)(2,1)}, u32[]{:S(2)}, u32[]{:S(2)}) %collective-permute-start.4) | collective-permute-done | bytes 270368 | tf_op jit(solution)/shard_map/grad_sum/ppermute | solution.py:435
  51.9 1.2 fusion.21
  54.0 7.9 %all-to-all-start = ((bf16[8,80,256]{2,1,0:T(8,128)(2,1)}), bf16[8,80,256]{2,1,0:T(8,128)(2,1)S(1)}, u32[]{:S(2)}, u32[]{:S(2)}) async-start(bf16[8,80,256]{2,1,0:T(8,128)(2,1)} %fusion.22.trigger), calls=%async_computation | async-start | bytes 655360 | tf_op jit(solution)/shard_map/grad_sum/all_to_all | solution.py:29
  61.9 14.7 %all-to-all-done = bf16[8,80,256]{2,1,0:T(8,128)(2,1)S(1)} async-done(((bf16[8,80,256]{2,1,0:T(8,128)(2,1)}), bf16[8,80,256]{2,1,0:T(8,128)(2,1)S(1)}, u32[]{:S(2)}, u32[]{:S(2)}) %all-to-all-start) | async-done | bytes 327712 | tf_op jit(solution)/shard_map/grad_sum/all_to_all | solution.py:29
  78.1 3.4 %all-to-all-start.1 = ((bf16[8,80,256]{2,1,0:T(8,128)(2,1)}), bf16[8,80,256]{2,1,0:T(8,128)(2,1)S(1)}, u32[]{:S(2)}, u32[]{:S(2)}) async-start(bf16[8,80,256]{2,1,0:T(8,128)(2,1)} %broadcast_in_dim.46), calls=%async_computation.1 | async-start | bytes 655360 | tf_op jit(solution)/shard_map/grad_all/all_to_all | solution.py:29
  81.6 5.1 %collective-permute-start.10 = (bf16[4,16,256]{2,1,0:T(8,128)(2,1)S(1)}, bf16[4,16,256]{2,1,0:T(8,128)(2,1)S(1)}, u32[]{:S(2)}, u32[]{:S(2)}) collective-permute-start(bf16[4,16,256]{2,1,0:T(8,128)(2,1)S(1)} %copy-done.35), channel_id=1, source_target_pairs={{0,4},{4,0},{1,5},{5,1},{2,6},{6,2},{3,7},{7,3},{8,12},{12,8},{9,1... | collective-permute-start | bytes 98312 | tf_op jit(solution)/shard_map/grad_sum/ppermute | solution.py:25
  86.7 0.9 collective-permute-done.10.other
  88.1 1.4 choose.1
  89.6 1.9 collective-permute-start.12
  91.6 0.9 collective-permute-start.11
  92.5 4.0 %collective-permute-done.11.refs_1_ = bf16[4,16,256]{2,1,0:T(8,128)(2,1)S(1)} collective-permute-done((bf16[4,16,256]{2,1,0:T(8,128)(2,1)}, bf16[4,16,256]{2,1,0:T(8,128)(2,1)S(1)}, u32[]{:S(2)}, u32[]{:S(2)}) %collective-permute-start.11) | collective-permute-done | bytes 32800 | tf_op jit(solution)/shard_map/grad_sum/ppermute | solution.py:33
  97.1 1.5 join.3
  98.9 1.5 collective-permute-start.14
  101.1 1.1 broadcast_in_dim.48
  102.2 3.5 %all-to-all-start.2 = ((bf16[4,512,256]{2,1,0:T(8,128)(2,1)}), bf16[4,512,256]{2,1,0:T(8,128)(2,1)S(1)}, u32[]{:S(2)}, u32[]{:S(2)}) async-start(bf16[4,512,256]{2,1,0:T(8,128)(2,1)} %broadcast_in_dim.48), calls=%async_computation.2 | async-start | bytes 2097152 | tf_op jit(solution)/shard_map/grad_all/all_to_all | solution.py:29
  108.9 1.4 stack.51.where
  110.3 1.7 copy-done.9
  112.1 2.4 %prep.1 = (bf16[1024,1024]{1,0:T(8,128)(2,1)S(1)}, bf16[1024,1024]{1,0:T(8,128)(2,1)S(1)}) custom-call(s32[9]{0:T(128)S(1)} %stack.51.where, bf16[8,40,16,256]{3,2,1,0:T(8,128)(2,1)S(1)} %bitcast.52, bf16[8,40,16,256]{3,2,1,0:T(8,128)(2,1)} %collective-permute-done.14.oth), custom_call_target="tpu_custom_call" | custom-call | flops 6000000000 | bytes 24000000 | tf_op jit(solution)/shard_map/grad_all/prep/pallas_call | solution.py:65
  114.5 1.3 copy-done.1
  115.9 1.3 copy-done.5
  117.2 3.7 %all-to-all-done.2.own = bf16[4,512,256]{2,1,0:T(8,128)(2,1)S(1)} async-done(((bf16[4,512,256]{2,1,0:T(8,128)(2,1)}), bf16[4,512,256]{2,1,0:T(8,128)(2,1)S(1)}, u32[]{:S(2)}, u32[]{:S(2)}) %all-to-all-start.2) | async-done | bytes 1048608 | tf_op jit(solution)/shard_map/grad_all/all_to_all | solution.py:29
  120.9 0.8 collective-permute-start.15
  121.7 2.3 %collective-permute-done.15.oth = bf16[4,512,256]{2,1,0:T(8,128)(2,1)S(1)} collective-permute-done((bf16[4,512,256]{2,1,0:T(8,128)(2,1)S(1)}, bf16[4,512,256]{2,1,0:T(8,128)(2,1)S(1)}, u32[]{:S(2)}, u32[]{:S(2)}) %collective-permute-start.15) | collective-permute-done | bytes 1048608 | tf_op jit(solution)/shard_map/grad_all/ppermute | solution.py:25
  124.0 1.6 copy-done.2
  125.6 1.6 copy-done.6
  127.2 1.8 copy-done.10
  129.0 5.3 %rotate.1 = (bf16[1024,1024]{1,0:T(8,128)(2,1)S(1)}, bf16[1024,1024]{1,0:T(8,128)(2,1)S(1)}, bf16[4,512,256]{2,1,0:T(8,128)(2,1)S(1)}, bf16[4,16,256]{2,1,0:T(8,128)(2,1)S(1)}) custom-call(s32[9]{0:T(128)S(1)} %stack.51.where, bf16[4,512,256]{2,1,0:T(8,128)(2,1)S(1)} %all-to-all-done.2.own, bf16[4,512,256]{2,1,0:T(8,128)(2,1)S(1)} %collective-permute-done.15.oth, ...), custom_call_target="tpu_custom_call" | custom-call | tf_op jit(solution)/shard_map/rotate/rotate/pallas_call | solution.py:65
  134.3 1.0 copy-done.11
  135.3 1.4 copy-done.16
  136.7 1.4 copy-done.18
  138.1 3.5 %all-to-all-start.3 = ((bf16[4,512,256]{2,1,0:T(8,128)(2,1)}), bf16[4,512,256]{2,1,0:T(8,128)(2,1)S(1)}, u32[]{:S(2)}, u32[]{:S(2)}) async-start(bf16[4,512,256]{2,1,0:T(8,128)(2,1)} %copy-done.11), calls=%async_computation.3 | async-start | bytes 2097152 | tf_op jit(solution)/shard_map/rotate/all_to_all | solution.py:29
  141.6 1.6 copy-done.3
  143.2 1.6 copy-done.7
  144.8 1.3 copy-done.20
  146.1 3.2 %old_power.1.old = f32[1024,1024]{1,0:T(8,128)S(1)} custom-call(s32[9]{0:T(128)S(1)} %stack.51.where, bf16[8,20,16,256]{3,2,1,0:T(8,128)(2,1)S(1)} %bitcast.55, bf16[1024,1024]{1,0:T(8,128)(2,1)S(1)} %copy-done.3, bf16[1024,1024]{1,0:T(8,128)(2,1)S(1)} %copy-done.7), custom_call_target="tpu_custom_call" | custom-call | flops 6000000000 | bytes 24000000 | tf_op jit(solution)/shard_map/power/old_power/pallas_call | solution.py:65
  149.4 6.9 %power.1 = (bf16[4,32,256]{2,1,0:T(8,128)(2,1)S(1)}, bf16[4,32,256]{2,1,0:T(8,128)(2,1)S(1)}) custom-call(s32[9]{0:T(128)S(1)} %stack.51.where, bf16[1024,1024]{1,0:T(8,128)(2,1)S(1)} %copy-done.17, bf16[1024,1024]{1,0:T(8,128)(2,1)S(1)} %copy-done.19, f32[1024,1024]{1,0:T(8,128)S(1)} %old_power.1.old), custom_call_target="tpu_custom_call" | custom-call | flops 6000000000 | bytes 24000000 | tf_op jit(solution)/shard_map/power/power/pallas_call | solution.py:65
  156.6 1.7 copy-done.8
  158.4 1.0 back.1.own
  159.9 1.2 collective-permute-done.16.oth
  161.0 1.2 update.1
  162.3 19.4 %all_to_all.25.got = bf16[4,608,256]{2,1,0:T(8,128)(2,1)S(1)} all-to-all(bf16[4,608,256]{2,1,0:T(8,128)(2,1)S(1)} %update.1), channel_id=1, replica_groups=mesh['x'=4,'z'=8,'c'=2,'mp'=4] {'x'}, dimensions={0} | all-to-all | bytes 2490368 | tf_op jit(solution)/shard_map/home/all_to_all | solution.py:29
  182.4 1.6 collective-permute-start.17
  184.0 1.3 collective-permute-done.17.recv
  185.3 1.5 final.1
  (105 shorter events, 10.3 us)
Async XLA Ops:
  7.2 9.6 %copy-start = (bf16[1024,4,256]{2,1,0:T(4,128)(2,1)S(1)}, bf16[1024,4,256]{2,1,0:T(4,128)(2,1)}, u32[]{:S(2)}) copy-start(bf16[1024,4,256]{2,1,0:T(4,128)(2,1)} %param.13) | copy-start | bytes 6291460
  7.2 91.7 %all-gather.5.cloned.1.call-start = ((), (), s32[]{:S(2)}) async-start(), calls=%async_computation.5 | async-start | bytes 2949120 | tf_op jit(solution)/shard_map/grad_sum/all_gather | solution.py:432
  9.1 10.2 %collective-permute-start = (bf16[6,16,256]{2,1,0:T(8,128)(2,1)}, bf16[6,16,256]{2,1,0:T(8,128)(2,1)S(1)}, u32[]{:S(2)}, u32[]{:S(2)}) collective-permute-start(bf16[6,16,256]{2,1,0:T(8,128)(2,1)} %get-tuple-element.56), channel_id=1, source_target_pairs={{0,64},{64,128},{128,192},{192,0},{1,65},{65,129},{129,193},{193,1... | collective-permute-start | bytes 147464 | tf_op jit(solution)/shard_map/state_rows/ppermute | solution.py:415
  11.2 8.1 %collective-permute-start.1 = (bf16[6,16,256]{2,1,0:T(8,128)(2,1)}, bf16[6,16,256]{2,1,0:T(8,128)(2,1)S(1)}, u32[]{:S(2)}, u32[]{:S(2)}) collective-permute-start(bf16[6,16,256]{2,1,0:T(8,128)(2,1)} %get-tuple-element.57), channel_id=1, source_target_pairs={{0,128},{64,192},{128,0},{192,64},{1,129},{65,193},{129,1},{193,65... | collective-permute-start | bytes 147464 | tf_op jit(solution)/shard_map/state_rows/ppermute | solution.py:415
  13.7 5.7 %collective-permute-start.2 = (bf16[6,16,256]{2,1,0:T(8,128)(2,1)}, bf16[6,16,256]{2,1,0:T(8,128)(2,1)S(1)}, u32[]{:S(2)}, u32[]{:S(2)}) collective-permute-start(bf16[6,16,256]{2,1,0:T(8,128)(2,1)} %get-tuple-element.58), channel_id=1, source_target_pairs={{0,192},{64,0},{128,64},{192,128},{1,193},{65,1},{129,65},{193,129... | collective-permute-start | bytes 147464 | tf_op jit(solution)/shard_map/state_rows/ppermute | solution.py:415
  19.4 4.2 %copy-start.25 = (bf16[6,16,256]{2,1,0:T(8,128)(2,1)}, bf16[6,16,256]{2,1,0:T(8,128)(2,1)S(1)}, u32[]{:S(2)}) copy-start(bf16[6,16,256]{2,1,0:T(8,128)(2,1)S(1)} %collective-permute-done.r1) | copy-start | bytes 147460
  19.4 4.2 %copy-start.26 = (bf16[6,16,256]{2,1,0:T(8,128)(2,1)}, bf16[6,16,256]{2,1,0:T(8,128)(2,1)S(1)}, u32[]{:S(2)}) copy-start(bf16[6,16,256]{2,1,0:T(8,128)(2,1)S(1)} %collective-permute-done.1.r2) | copy-start | bytes 147460
  19.4 4.1 %copy-start.27 = (bf16[6,16,256]{2,1,0:T(8,128)(2,1)}, bf16[6,16,256]{2,1,0:T(8,128)(2,1)S(1)}, u32[]{:S(2)}) copy-start(bf16[6,16,256]{2,1,0:T(8,128)(2,1)S(1)} %collective-permute-done.2.r3) | copy-start | bytes 147460
  19.4 4.1 %collective-permute-start.3 = (bf16[4,528,256]{2,1,0:T(8,128)(2,1)S(1)}, bf16[4,528,256]{2,1,0:T(8,128)(2,1)}, u32[]{:S(2)}, u32[]{:S(2)}) collective-permute-start(bf16[4,528,256]{2,1,0:T(8,128)(2,1)S(1)} %pad_maximum_fusion), channel_id=1, source_target_pairs={{0,4},{4,0},{1,5},{5,1},{2,6},{6,2},{3,7},{7,3},{8,12},{12,8},{9,1... | collective-permute-start | bytes 3244040 | tf_op jit(solution)/shard_map/grad_sum/ppermute | solution.py:25
  26.1 11.6 %copy-start.21 = (bf16[4,528,256]{2,1,0:T(8,128)(2,1)S(1)}, bf16[4,528,256]{2,1,0:T(8,128)(2,1)}, u32[]{:S(2)}) copy-start(bf16[4,528,256]{2,1,0:T(8,128)(2,1)} %fusion.trigger) | copy-start | bytes 3244036
  27.7 5.0 %collective-permute-start.7 = (bf16[8,16,256]{2,1,0:T(8,128)(2,1)}, bf16[8,16,256]{2,1,0:T(8,128)(2,1)S(1)}, u32[]{:S(2)}, u32[]{:S(2)}) collective-permute-start(bf16[8,16,256]{2,1,0:T(8,128)(2,1)} %get-tuple-element.64.refs_0_), channel_id=1, source_target_pairs={{0,1},{1,2},{2,3},{3,0},{4,5},{5,6},{6,7},{7,4},{8,9},{9,10},{10,1... | collective-permute-start | bytes 196616 | tf_op jit(solution)/shard_map/grad_sum/ppermute | solution.py:33
  29.0 5.9 %collective-permute-start.8 = (bf16[8,16,256]{2,1,0:T(8,128)(2,1)}, bf16[8,16,256]{2,1,0:T(8,128)(2,1)S(1)}, u32[]{:S(2)}, u32[]{:S(2)}) collective-permute-start(bf16[8,16,256]{2,1,0:T(8,128)(2,1)} %get-tuple-element.64.refs_0_), channel_id=1, source_target_pairs={{0,2},{1,3},{2,0},{3,1},{4,6},{5,7},{6,4},{7,5},{8,10},{9,11},{10,... | collective-permute-start | bytes 196616 | tf_op jit(solution)/shard_map/grad_sum/ppermute | solution.py:33
  31.7 3.6 %collective-permute-start.9 = (bf16[8,16,256]{2,1,0:T(8,128)(2,1)}, bf16[8,16,256]{2,1,0:T(8,128)(2,1)S(1)}, u32[]{:S(2)}, u32[]{:S(2)}) collective-permute-start(bf16[8,16,256]{2,1,0:T(8,128)(2,1)} %get-tuple-element.64.refs_0_), channel_id=1, source_target_pairs={{0,3},{1,0},{2,1},{3,2},{4,7},{5,4},{6,5},{7,6},{8,11},{9,8},{10,9... | collective-permute-start | bytes 196616 | tf_op jit(solution)/shard_map/grad_sum/ppermute | solution.py:33
  32.7 2.6 %copy-start.22 = (bf16[8,16,256]{2,1,0:T(8,128)(2,1)}, bf16[8,16,256]{2,1,0:T(8,128)(2,1)S(1)}, u32[]{:S(2)}) copy-start(bf16[8,16,256]{2,1,0:T(8,128)(2,1)S(1)} %collective-permute-done.7.refs_1_) | copy-start | bytes 196612
  34.9 0.6 copy-start.23
  35.3 0.6 copy-start.24
  38.6 38.1 %copy-start.33 = (f32[32]{0:T(128)S(1)}, f32[32]{0:T(128)}, u32[]{:S(2)}) copy-start(f32[32]{0:T(128)} %param.22) | copy-start | bytes 388
  38.6 38.1 %copy-start.34 = (f32[32]{0:T(128)S(1)}, f32[32]{0:T(128)}, u32[]{:S(2)}) copy-start(f32[32]{0:T(128)} %param.23) | copy-start | bytes 388
  38.6 6.5 %collective-permute-start.6 = (bf16[528,256]{1,0:T(8,128)(2,1)}, bf16[528,256]{1,0:T(8,128)(2,1)S(1)}, u32[]{:S(2)}, u32[]{:S(2)}) collective-permute-start(bf16[528,256]{1,0:T(8,128)(2,1)} %get-tuple-element.108), channel_id=1, source_target_pairs={{0,192},{64,0},{128,64},{192,128},{1,193},{65,1},{129,65},{193,129... | collective-permute-start | bytes 811016 | tf_op jit(solution)/shard_map/grad_sum/ppermute | solution.py:435
  39.2 8.1 %collective-permute-start.5 = (bf16[528,256]{1,0:T(8,128)(2,1)}, bf16[528,256]{1,0:T(8,128)(2,1)}, u32[]{:S(2)}, u32[]{:S(2)}) collective-permute-start(bf16[528,256]{1,0:T(8,128)(2,1)} %get-tuple-element.109), channel_id=1, source_target_pairs={{0,64},{64,128},{128,192},{192,0},{1,65},{65,129},{129,193},{193,1... | collective-permute-start | bytes 811016 | tf_op jit(solution)/shard_map/grad_sum/ppermute | solution.py:435
  40.1 11.9 %collective-permute-start.4 = (bf16[528,256]{1,0:T(8,128)(2,1)}, bf16[528,256]{1,0:T(8,128)(2,1)}, u32[]{:S(2)}, u32[]{:S(2)}) collective-permute-start(bf16[528,256]{1,0:T(8,128)(2,1)} %get-tuple-element.107), channel_id=1, source_target_pairs={{0,128},{64,192},{128,0},{192,64},{1,129},{65,193},{129,1},{193,65... | collective-permute-start | bytes 811016 | tf_op jit(solution)/shard_map/grad_sum/ppermute | solution.py:435
  41.0 40.6 %copy-start.35 = (bf16[4,16,256]{2,1,0:T(8,128)(2,1)S(1)}, bf16[4,16,256]{2,1,0:T(8,128)(2,1)}, u32[]{:S(2)}) copy-start(bf16[4,16,256]{2,1,0:T(8,128)(2,1)} %get-tuple-element.67) | copy-start | bytes 98308
  53.1 47.3 %copy-start.32 = (s32[5]{0:T(128)S(1)}, s32[5]{0:T(128)}, u32[]{:S(2)}) copy-start(s32[5]{0:T(128)} %param.15) | copy-start | bytes 64
  54.0 22.6 %all-to-all-start = ((bf16[8,80,256]{2,1,0:T(8,128)(2,1)}), bf16[8,80,256]{2,1,0:T(8,128)(2,1)S(1)}, u32[]{:S(2)}, u32[]{:S(2)}) async-start(bf16[8,80,256]{2,1,0:T(8,128)(2,1)} %fusion.22.trigger), calls=%async_computation | async-start | bytes 655360 | tf_op jit(solution)/shard_map/grad_sum/all_to_all | solution.py:29
  78.1 20.6 %all-to-all-start.1 = ((bf16[8,80,256]{2,1,0:T(8,128)(2,1)}), bf16[8,80,256]{2,1,0:T(8,128)(2,1)S(1)}, u32[]{:S(2)}, u32[]{:S(2)}) async-start(bf16[8,80,256]{2,1,0:T(8,128)(2,1)} %broadcast_in_dim.46), calls=%async_computation.1 | async-start | bytes 655360 | tf_op jit(solution)/shard_map/grad_all/all_to_all | solution.py:29
  81.5 60.1 %all-gather.7.cloned.1.call-start = ((), (), s32[]{:S(2)}) async-start(), calls=%async_computation.6 | async-start | bytes 1474560 | tf_op jit(solution)/shard_map/grad_all/all_gather | solution.py:462
  81.6 5.9 %collective-permute-start.10 = (bf16[4,16,256]{2,1,0:T(8,128)(2,1)S(1)}, bf16[4,16,256]{2,1,0:T(8,128)(2,1)S(1)}, u32[]{:S(2)}, u32[]{:S(2)}) collective-permute-start(bf16[4,16,256]{2,1,0:T(8,128)(2,1)S(1)} %copy-done.35), channel_id=1, source_target_pairs={{0,4},{4,0},{1,5},{5,1},{2,6},{6,2},{3,7},{7,3},{8,12},{12,8},{9,1... | collective-permute-start | bytes 98312 | tf_op jit(solution)/shard_map/grad_sum/ppermute | solution.py:25
  87.5 0.6 copy-start.31
  89.6 6.9 %collective-permute-start.12 = (bf16[4,16,256]{2,1,0:T(8,128)(2,1)}, bf16[4,16,256]{2,1,0:T(8,128)(2,1)S(1)}, u32[]{:S(2)}, u32[]{:S(2)}) collective-permute-start(bf16[4,16,256]{2,1,0:T(8,128)(2,1)} %get-tuple-element.70), channel_id=1, source_target_pairs={{0,3},{1,0},{2,1},{3,2},{4,7},{5,4},{6,5},{7,6},{8,11},{9,8},{10,9... | collective-permute-start | bytes 98312 | tf_op jit(solution)/shard_map/grad_sum/ppermute | solution.py:33
  91.4 5.0 %collective-permute-start.13 = (bf16[4,16,256]{2,1,0:T(8,128)(2,1)}, bf16[4,16,256]{2,1,0:T(8,128)(2,1)S(1)}, u32[]{:S(2)}, u32[]{:S(2)}) collective-permute-start(bf16[4,16,256]{2,1,0:T(8,128)(2,1)} %get-tuple-element.70), channel_id=1, source_target_pairs={{0,2},{1,3},{2,0},{3,1},{4,6},{5,7},{6,4},{7,5},{8,10},{9,11},{10,... | collective-permute-start | bytes 98312 | tf_op jit(solution)/shard_map/grad_sum/ppermute | solution.py:33
  91.6 4.8 %collective-permute-start.11 = (bf16[4,16,256]{2,1,0:T(8,128)(2,1)}, bf16[4,16,256]{2,1,0:T(8,128)(2,1)S(1)}, u32[]{:S(2)}, u32[]{:S(2)}) collective-permute-start(bf16[4,16,256]{2,1,0:T(8,128)(2,1)} %get-tuple-element.69), channel_id=1, source_target_pairs={{0,1},{1,2},{2,3},{3,0},{4,5},{5,6},{6,7},{7,4},{8,9},{9,10},{10,1... | collective-permute-start | bytes 98312 | tf_op jit(solution)/shard_map/grad_sum/ppermute | solution.py:33
  96.5 0.6 copy-start.30
  96.5 0.6 copy-start.28
  96.5 0.6 copy-start.29
  98.9 11.5 %collective-permute-start.14 = (bf16[8,40,16,256]{3,2,1,0:T(8,128)(2,1)}, bf16[8,40,16,256]{3,2,1,0:T(8,128)(2,1)}, u32[]{:S(2)}, u32[]{:S(2)}) collective-permute-start(bf16[8,40,16,256]{3,2,1,0:T(8,128)(2,1)} %bitcast.51), channel_id=1, source_target_pairs={{0,4},{4,0},{1,5},{5,1},{2,6},{6,2},{3,7},{7,3},{8,12},{12,8},{9,1... | collective-permute-start | bytes 7864328 | tf_op jit(solution)/shard_map/grad_all/ppermute | solution.py:25
  102.2 18.7 %all-to-all-start.2 = ((bf16[4,512,256]{2,1,0:T(8,128)(2,1)}), bf16[4,512,256]{2,1,0:T(8,128)(2,1)S(1)}, u32[]{:S(2)}, u32[]{:S(2)}) async-start(bf16[4,512,256]{2,1,0:T(8,128)(2,1)} %broadcast_in_dim.48), calls=%async_computation.2 | async-start | bytes 2097152 | tf_op jit(solution)/shard_map/grad_all/all_to_all | solution.py:29
  110.3 1.7 copy-start.9
  114.5 1.4 copy-start.1
  115.9 1.3 copy-start.5
  120.9 3.1 %collective-permute-start.15 = (bf16[4,512,256]{2,1,0:T(8,128)(2,1)S(1)}, bf16[4,512,256]{2,1,0:T(8,128)(2,1)S(1)}, u32[]{:S(2)}, u32[]{:S(2)}) collective-permute-start(bf16[4,512,256]{2,1,0:T(8,128)(2,1)S(1)} %all-to-all-done.2.own), channel_id=1, source_target_pairs={{0,4},{4,0},{1,5},{5,1},{2,6},{6,2},{3,7},{7,3},{8,12},{12,8},{9,1... | collective-permute-start | bytes 3145736 | tf_op jit(solution)/shard_map/grad_all/ppermute | solution.py:25
  124.0 1.6 copy-start.2
  125.6 1.6 copy-start.6
  127.2 1.8 copy-start.10
  134.3 1.0 copy-start.11
  135.3 1.4 copy-start.16
  136.7 1.4 copy-start.18
  138.1 18.6 %all-to-all-start.3 = ((bf16[4,512,256]{2,1,0:T(8,128)(2,1)}), bf16[4,512,256]{2,1,0:T(8,128)(2,1)S(1)}, u32[]{:S(2)}, u32[]{:S(2)}) async-start(bf16[4,512,256]{2,1,0:T(8,128)(2,1)} %copy-done.11), calls=%async_computation.3 | async-start | bytes 2097152 | tf_op jit(solution)/shard_map/rotate/all_to_all | solution.py:29
  141.6 1.6 copy-start.3
  143.2 1.6 copy-start.7
  144.8 1.3 copy-start.20
  146.1 3.2 %copy-start.17 = (bf16[1024,1024]{1,0:T(8,128)(2,1)S(1)}, bf16[1024,1024]{1,0:T(8,128)(2,1)}, u32[]{:S(2)}) copy-start(bf16[1024,1024]{1,0:T(8,128)(2,1)} %copy-done.16) | copy-start | bytes 6291460
  146.1 3.2 %copy-start.19 = (bf16[1024,1024]{1,0:T(8,128)(2,1)S(1)}, bf16[1024,1024]{1,0:T(8,128)(2,1)}, u32[]{:S(2)}) copy-start(bf16[1024,1024]{1,0:T(8,128)(2,1)} %copy-done.18) | copy-start | bytes 6291460
  156.6 4.4 %copy-start.4 = (bf16[1024,1024]{1,0:T(8,128)(2,1)S(1)}, bf16[1024,1024]{1,0:T(8,128)(2,1)}, u32[]{:S(2)}) copy-start(bf16[1024,1024]{1,0:T(8,128)(2,1)} %copy-done.1) | copy-start | bytes 6291460
  156.6 1.7 copy-start.8
  159.4 1.6 collective-permute-start.16
  162.3 23.0 %copy-start.12 = (f32[4,16,256]{2,1,0:T(8,128)S(1)}, f32[4,16,256]{2,1,0:T(8,128)}, u32[]{:S(2)}) copy-start(f32[4,16,256]{2,1,0:T(8,128)} %m1.1) | copy-start | bytes 196612
  162.3 22.9 %copy-start.13 = (f32[4,16,256]{2,1,0:T(8,128)S(1)}, f32[4,16,256]{2,1,0:T(8,128)}, u32[]{:S(2)}) copy-start(f32[4,16,256]{2,1,0:T(8,128)} %m2.1) | copy-start | bytes 196612
  162.3 22.9 %copy-start.14 = (f32[4,16,256]{2,1,0:T(8,128)S(1)}, f32[4,16,256]{2,1,0:T(8,128)}, u32[]{:S(2)}) copy-start(f32[4,16,256]{2,1,0:T(8,128)} %sl.1) | copy-start | bytes 196612
  162.3 22.9 %copy-start.15 = (f32[4,16,256]{2,1,0:T(8,128)S(1)}, f32[4,16,256]{2,1,0:T(8,128)}, u32[]{:S(2)}) copy-start(f32[4,16,256]{2,1,0:T(8,128)} %sr.1) | copy-start | bytes 196612
  182.4 2.9 %collective-permute-start.17 = (bf16[656,256]{1,0:T(8,128)(2,1)S(1)}, bf16[656,256]{1,0:T(8,128)(2,1)S(1)}, u32[]{:S(2)}, u32[]{:S(2)}) collective-permute-start(bf16[656,256]{1,0:T(8,128)(2,1)S(1)} %get-tuple-element.91), channel_id=1, source_target_pairs={{0,4},{4,0},{1,5},{5,1},{2,6},{6,2},{3,7},{7,3},{8,12},{12,8},{9,1... | collective-permute-start | bytes 1007624 | tf_op jit(solution)/shard_map/home/ppermute | solution.py:25
Sparse Core Ops, SparseCore 0:
  37.8 49.0 all-gather.4
  100.5 33.8 all-gather.6
